TPU v7x, 32 devices: a whole 2x2x4 slice. The times are simulated.
32 devices in a mesh: peer: 4 (over y, x), space: 8 (over z, core).
Axes of the slice: x: 2, y: 2, z: 4, core: 2. Of those that a mesh axis runs over, the one named last changes fastest.
Arguments:
- images: bfloat16 [4, 128, 32, 512], P('peer', 'space'), may hold values from -6 to 6
- task_grad: bfloat16 [4, 128, 32, 512], P('peer', 'space'), may hold values from -6 to 6
- pairing: int32 [4], replicated, may hold values from 0 to 3, as said below
- first_kernel: bfloat16 [4, 3, 3, 512, 512], P('peer'), may hold values from -0.09375 to 0.09375
- first_scale: float32 [4, 512], P('peer'), may hold values from 0.25 to 1.75
- first_shift: float32 [4, 512], P('peer'), may hold values from -3 to 3
- second_kernel: bfloat16 [4, 3, 3, 512, 512], P('peer'), may hold values from -0.09375 to 0.09375
- second_scale: float32 [4, 512], P('peer'), may hold values from 0.25 to 1.75
- second_shift: float32 [4, 512], P('peer'), may hold values from -3 to 3
Outputs:
- input_grad: bfloat16 [4, 128, 32, 512], P('peer', 'space')
Inputs may be any that keep to these rules, and one draw needn't show every extreme that they name: `pairing`: every network index appears exactly once.
All inputs are finite; a program needn't handle non-finite values.
Results may differ from a plain program's by a relative error of at most 0.012.
Values may be sent and summed in bfloat16 or wider, within the bound.
No kernel may reach another device: no remote copies, remote signals or barrier semaphores. Data moves between devices by JAX's collectives and lax.ppermute only.
A program may use at most 64 MiB of HBM per device.

v0:
```python
import functools
import itertools
import math

import jax
import jax.numpy as jnp
from jax import lax
from jax.experimental import pallas as pl
from jax.experimental.pallas import tpu as pltpu
from jax.sharding import PartitionSpec as P

BF16 = jnp.bfloat16
F32 = jnp.float32
VMEM_LIMIT = 40 * 2**20
MAX_ROUTES = 24
LULL = 30
D1 = 2
D2 = 4
EDGE = D1 + D2


def side():
    return lax.rem(lax.axis_index("space"), 2)


def at_end():
    me = lax.axis_index("space")
    return jnp.logical_or(me == 0, me == lax.axis_size("space") - 1)


def pick(odd, if_even, if_odd):
    return if_even + odd * (if_odd - if_even)


def put(cat, start, rows, value, dilation):
    width, chans = value.shape[1], value.shape[2]
    none = jnp.zeros((rows, dilation, chans), value.dtype)
    at = pl.ds(start, rows)
    cat[at, :, 0:chans] = jnp.concatenate([none, value[:, : width - dilation]], axis=1)
    cat[at, :, chans : 2 * chans] = value
    cat[at, :, 2 * chans : 3 * chans] = jnp.concatenate([value[:, dilation:], none], axis=1)


def no_wait(*tap):
    pass


def conv(cat, kernel, dilation, rows, lo, size):
    width, depth = cat.shape[1], cat.shape[2]
    total = None
    for a in range(3):
        block = cat[a * dilation : a * dilation + rows].reshape(rows * width, depth)
        part = jnp.dot(block, kernel[a, :, lo : lo + size], preferred_element_type=F32)
        total = part if total is None else total + part
    return total


def conv_t(cat, kernel, dilation, rows, lo, size):
    width, chans = cat.shape[1], cat.shape[2] // 3
    total = None
    for a in range(3):
        for b in range(3):
            block = cat[(2 - a) * dilation : (2 - a) * dilation + rows, :, (2 - b) * chans : (3 - b) * chans]
            part = lax.dot_general(
                block.reshape(rows * width, chans),
                kernel[a, b * chans + lo : b * chans + lo + size],
                (((1,), (1,)), ((), ())),
                preferred_element_type=F32,
            )
            total = part if total is None else total + part
    return total


def hide_beyond(rim, odd, count):
    @pl.when(at_end())
    def _():
        none = jnp.zeros((count,) + rim.shape[1:], rim.dtype)
        rim[pl.ds(pick(odd, 0, rim.shape[0] - count), count)] = none


def put_far(cat, start, halo, dilation):
    rows = halo.shape[0]
    put(cat, start, rows, halo[...], dilation)

    @pl.when(at_end())
    def _():
        cat[pl.ds(start, rows)] = jnp.zeros((rows,) + cat.shape[1:], cat.dtype)


def halves(chans):
    step = chans // 2 if chans % 256 == 0 else chans
    return [(lo, step) for lo in range(0, chans, step)]


def conv_act(cat, kernel, scale, shift, dilation, act, slope):
    rows, width, chans = act.shape
    for lo, size in halves(chans):
        cut = slice(lo, lo + size)
        pre = conv(cat, kernel, dilation, rows, lo, size) * scale[:, cut] + shift[:, cut]
        sig = 1.0 / (1.0 + jnp.exp(-pre))
        act[:, :, cut] = (pre * sig).astype(BF16).reshape(rows, width, size)
        slope[:, :, cut] = (sig * (1.0 + pre * (1.0 - sig)) * scale[:, cut]).reshape(rows, width, size)


def prepare(
    image, scale1, shift1, scale2, shift2, pairing, index, strip, near_send, far_send, vectors, pair, sems, *, table
):
    copies = [
        pltpu.make_async_copy(image, strip, sems.at[0]),
        pltpu.make_async_copy(pairing, pair, sems.at[1]),
    ]
    for i, source in enumerate((scale1, shift1, scale2, shift2)):
        copies.append(pltpu.make_async_copy(source, vectors.at[pl.ds(8 * i, 1)], sems.at[2 + i]))
    for copy in copies:
        copy.start()
    copies[1].wait()
    rank = jnp.int32(0)
    if table:
        groups = pair.shape[0]
        for i in range(groups):
            smaller = jnp.int32(0)
            for j in range(i + 1, groups):
                smaller = smaller + (pair[j] < pair[i]).astype(jnp.int32)
            rank = rank + smaller * math.factorial(groups - 1 - i)
        rank = lookup(rank, table)
    index[0] = rank
    me = lax.axis_index("peer")
    paired = jnp.where(pair[me] == me, 0.0, 1.0)
    vectors[pl.ds(32, 1)] = jnp.full((1, vectors.shape[1]), paired, F32)
    odd = side()
    edge = near_send.shape[0]
    last = strip.shape[0] - edge
    copies[0].wait()
    near_send[...] = strip[pl.ds(pick(odd, last, 0), edge)]
    far_send[...] = strip[pl.ds(pick(odd, 0, last), edge)]
    for copy in copies[2:]:
        copy.wait()


def first(image, near, kernel1, vectors, hidden, slope, cat):
    odd = side()
    strip, edge = image.shape[0], near.shape[0]
    put(cat, pick(odd, 0, edge), strip, image[...], D1)
    put(cat, pick(odd, strip, 0), edge, near[...], D1)
    conv_act(cat, kernel1, vectors[0:1], vectors[8:9], D1, hidden, slope)


def second(
    image, far, hidden, slope, kernel1, kernel2, vectors, task,
    feat_far, base_far, rate_far, feat_near, base_near, rate_near, fold,
    cat1, cat2, rim, slope1, slope2, part, feat, sems
):
    odd = side()
    strip, edge, held = image.shape[0], far.shape[0], hidden.shape[0]
    most = held - D1
    copies = [
        pltpu.make_async_copy(task, part, sems.at[0]),
        pltpu.make_async_copy(
            slope.at[pl.ds(pick(odd, 0, D1), most)], fold.at[pl.ds(pick(odd, D2, 0), most)], sems.at[1]
        ),
        pltpu.make_async_copy(
            slope1.at[pl.ds(pick(odd, D1, 0), D2)], fold.at[pl.ds(pick(odd, 0, most), D2)], sems.at[2]
        ),
    ]
    copies[0].start()
    copies[1].start()
    own = 2 * D1
    put_far(cat1, pick(odd, 0, own), far, D1)
    put(cat1, pick(odd, edge, 0), own, image[pl.ds(pick(odd, 0, strip - own), own)], D1)
    conv_act(cat1, kernel1, vectors[0:1], vectors[8:9], D1, rim, slope1)
    copies[2].start()
    hide_beyond(rim, odd, D2)
    put(cat2, pick(odd, edge, 0), held, hidden[...], D2)
    put(cat2, pick(odd, 0, held), edge, rim[...], D2)
    conv_act(cat2, kernel2, vectors[16:17], vectors[24:25], D2, feat, slope2)
    for copy in copies:
        copy.wait()
    paired = vectors[32:33]
    far_at = pl.ds(pick(odd, 0, strip - edge), edge)
    near_at = pl.ds(pick(odd, edge, 0), strip - edge)
    for at, own, base, rate in ((far_at, feat_far, base_far, rate_far), (near_at, feat_near, base_near, rate_near)):
        own[...] = feat[at]
        rate[...] = slope2[at] * paired
        base[...] = (part[at].astype(F32) + feat[at].astype(F32) * paired) * slope2[at]


def gradient(base, rate, partner, grad):
    def step(row, carry):
        grad[row] = (base[row] - partner[row].astype(F32) * rate[row]).astype(BF16)
        return carry

    lax.fori_loop(0, grad.shape[0], step, 0, unroll=2)


def grad_rest(base, rate, partner, grad_far, far, grads, near_send):
    odd = side()
    rows, edge = partner.shape[0], grad_far.shape[0]
    gradient(base, rate, partner, grads.at[pl.ds(pick(odd, 2 * edge, 0), rows)])
    grads[pl.ds(pick(odd, edge, rows), edge)] = grad_far[...]
    beyond = pl.ds(pick(odd, 0, edge + rows), edge)
    grads[beyond] = far[...]

    @pl.when(at_end())
    def _():
        grads[beyond] = jnp.zeros(far.shape, far.dtype)

    near_send[...] = grads[pl.ds(pick(odd, edge + rows, 0), edge)]


def bring(kernel2, kernel1, fold, kept2, kept1, slope, sems):
    pairs = ((kernel2, kept2), (kernel1, kept1), (fold, slope))
    copies = [pltpu.make_async_copy(source, target, sems.at[i]) for i, (source, target) in enumerate(pairs)]
    for copy in copies:
        copy.start()
    for copy in copies:
        copy.wait()


def backward(near, grads, fold, kernel2, kernel1, out, cat2, cat1, grad1):
    odd = side()
    edge, held, width, rows = near.shape[0], grads.shape[0], near.shape[1], grad1.shape[0]
    put(cat2, pick(odd, held, 0), edge, near[...], D2)
    put(cat2, pick(odd, 0, edge), held, grads[...], D2)
    for lo, size in halves(grad1.shape[2]):
        cut = slice(lo, lo + size)
        back = conv_t(cat2, kernel2, D2, rows, lo, size).reshape(rows, width, size)
        grad1[:, :, cut] = (back * fold[:, :, cut]).astype(BF16)
    hide_beyond(grad1, odd, D1)
    put(cat1, 0, rows, grad1[...], D1)
    rows = out.shape[0]
    for lo, size in halves(out.shape[2]):
        back = conv_t(cat1, kernel1, D1, rows, lo, size)
        out[:, :, lo : lo + size] = back.astype(BF16).reshape(rows, width, size)


def call(body, name, args, outs, scratch=(), flops=0, remote=(), stored=(), result=None):
    kinds = [pltpu.HBM if i in remote else pltpu.VMEM for i in range(len(args))]
    out_kinds = [
        pltpu.HBM if i in stored else pltpu.SMEM if o.dtype == jnp.int32 else pltpu.VMEM for i, o in enumerate(outs)
    ]
    return pl.pallas_call(
        body,
        out_shape=[o if i == result else k(o.shape, o.dtype) for i, (o, k) in enumerate(zip(outs, out_kinds))],
        in_specs=[pl.BlockSpec(memory_space=k) for k in kinds],
        out_specs=[pl.BlockSpec(memory_space=k) for k in out_kinds],
        scratch_shapes=[pltpu.VMEM(s.shape, s.dtype) if isinstance(s, jax.ShapeDtypeStruct) else s for s in scratch],
        compiler_params=pltpu.CompilerParams(vmem_limit_bytes=VMEM_LIMIT),
        cost_estimate=pl.CostEstimate(flops=flops, bytes_accessed=0, transcendentals=0),
        name=name,
    )(*[pltpu.with_memory_space_constraint(a, k) for a, k in zip(args, kinds)])


def routes_of(groups):
    pairings = list(itertools.permutations(range(groups)))
    moves = [frozenset((p, n) for n, p in enumerate(pair) if p != n) for pair in pairings]
    routes = []
    for move in sorted(set(moves), key=lambda m: (-len(m), sorted(m))):
        if not any(move <= route for route in routes):
            routes.append(move)
    chosen = [next(i for i, route in enumerate(routes) if move <= route) for move in moves]
    return [sorted(route) for route in routes], chosen


def spread(route, groups, space):
    moved = {source: target for source, target in route}
    return [
        (p * space + i, moved[p] * space + i if p in moved else p * space + (i ^ 1))
        for p in range(groups)
        for i in range(space)
    ]


def lookup(index, table):
    value = jnp.int32(table[0])
    for i in range(1, len(table)):
        if table[i] != table[i - 1]:
            value = jnp.where(index >= i, jnp.int32(table[i]), value)
    return value


def far_side(group, place, groups, space):
    other = place + 1 if place % 2 else place - 1
    if 0 <= other < space:
        return group * space + other
    return (group ^ 1) * space + place if groups % 2 == 0 else group * space + other % space


def swap_blocks(feat, pairing):
    groups = lax.axis_size("peer")
    chans = feat.shape[-1]
    blocks = feat.reshape(groups, feat.size // chans // groups, chans)
    received = lax.all_to_all(blocks, "peer", split_axis=0, concat_axis=0, tiled=True)
    chosen = jnp.take(received, pairing, axis=0)
    returned = lax.all_to_all(chosen, "peer", split_axis=0, concat_axis=0, tiled=True)
    return returned.reshape(feat.shape)


def per_device(images, task_grad, pairing, first_kernel, scale1, shift1, second_kernel, scale2, shift2):
    image, task = images[0], task_grad[0]
    strip, width, chans = image.shape
    kernel1 = first_kernel[0].reshape(3, 3 * chans, chans)
    kernel2 = second_kernel[0].reshape(3, 3 * chans, chans)
    space, groups = lax.axis_size("space"), lax.axis_size("peer")
    pairs = [(i, i ^ 1) for i in range(space)]
    across = [(p * space + i, far_side(p, i, groups, space)) for p in range(groups) for i in range(space)]
    per_row = 2 * 9 * width * chans * chans
    deep = strip + EDGE - 2 * D1

    def rows_of(count, kind=BF16):
        return jax.ShapeDtypeStruct((count, width, chans), kind)

    def cat_of(count):
        return jax.ShapeDtypeStruct((count, width, 3 * chans), BF16)

    def near(rows):
        return lax.ppermute(rows, "space", pairs)

    def far(rows):
        return lax.ppermute(rows, ("peer", "space"), across)

    routed = math.factorial(groups) <= MAX_ROUTES
    routes, chosen = routes_of(groups) if routed else ((), ())
    dma = pltpu.SemaphoreType.DMA
    index, image, near_send, far_send, vectors = call(
        functools.partial(prepare, table=tuple(chosen)),
        "prepare",
        (image, scale1, shift1, scale2, shift2, pairing),
        (
            jax.ShapeDtypeStruct((1,), jnp.int32),
            rows_of(strip),
            rows_of(EDGE),
            rows_of(EDGE),
            jax.ShapeDtypeStruct((40, chans), F32),
        ),
        (pltpu.SMEM((groups,), jnp.int32), dma((6,))),
        flops=LULL * per_row * strip,
        remote=range(6),
    )
    near_halo = near(near_send)
    far_halo = far(far_send)
    hidden, slope1 = call(
        first,
        "first",
        (image, near_halo, kernel1, vectors),
        (rows_of(deep), rows_of(deep, F32)),
        (cat_of(strip + EDGE),),
        flops=per_row * deep,
    )
    inner = strip - EDGE
    *given, fold = call(
        second,
        "second",
        (image, far_halo, hidden, slope1, kernel1, kernel2, vectors, task),
        (
            rows_of(EDGE),
            rows_of(EDGE, F32),
            rows_of(EDGE, F32),
            rows_of(inner),
            rows_of(inner, F32),
            rows_of(inner, F32),
            rows_of(strip + 2 * D1, F32),
        ),
        (
            cat_of(EDGE + 2 * D1),
            cat_of(strip + 2 * D2),
            rows_of(EDGE),
            rows_of(EDGE, F32),
            rows_of(strip, F32),
            rows_of(strip),
            rows_of(strip),
            dma((3,)),
        ),
        flops=per_row * (EDGE + strip),
        remote=(7,),
        stored=(6,),
    )

    whole = jax.ShapeDtypeStruct(kernel1.shape, BF16)

    def exchange(swap, feat_far, base_far, rate_far, feat_near, base_near, rate_near, *stored):
        partner_far = swap(feat_far)
        partner_near = swap(feat_near)
        (grad_far,) = call(gradient, "grad_far", (base_far, rate_far, partner_far), (rows_of(EDGE),))
        far_grad = far(grad_far)
        grads, near_send = call(
            grad_rest,
            "grad_rest",
            (base_near, rate_near, partner_near, grad_far, far_grad),
            (rows_of(strip + EDGE), rows_of(EDGE)),
        )
        brought = call(
            bring, "bring", stored, (whole, whole, rows_of(strip + 2 * D1, F32)), (dma((3,)),), remote=range(3)
        )
        return grads, near_send, *brought

    if routed:
        moves = [
            functools.partial(lax.ppermute, axis_name=("peer", "space"), perm=spread(route, groups, space))
            for route in routes
        ]
        state = lax.switch(index[0], [functools.partial(exchange, move) for move in moves], *given, kernel2, kernel1, fold)
    else:
        state = exchange(functools.partial(swap_blocks, pairing=pairing), *given, kernel2, kernel1, fold)
    grads, near_send, kernel2, kernel1, fold = state
    near_grad = near(near_send)
    back = strip + 2 * D1
    (out,) = call(
        backward,
        "backward",
        (near_grad, grads, fold, kernel2, kernel1),
        (rows_of(strip),),
        (cat_of(strip + 2 * EDGE), cat_of(back), rows_of(back)),
        flops=per_row * (back + strip),
        result=0,
    )
    return out[None]


def solution(mesh):
    placed = (
        P("peer", "space", None, None),
        P("peer", "space", None, None),
        P(),
        P("peer", None, None, None, None),
        P("peer", None),
        P("peer", None),
        P("peer", None, None, None, None),
        P("peer", None),
        P("peer", None),
    )
    return jax.shard_map(
        per_device,
        mesh=mesh,
        in_specs=placed,
        out_specs=P("peer", "space", None, None),
        check_vma=False,
    )
```

profile of v0, /device:TPU:1, one launch (start us, length us, event | category | flops | bytes accessed | tf_op | source)
XLA Modules:
  0.0 38.6 jit_solution(17567828263298657318)
XLA Ops:
  0.0 0.0 copy-start
  0.0 1.3 %prepare.1 = (s32[1]{0:T(128)S(4)}, bf16[16,32,512]{2,1,0:T(8,128)(2,1)S(1)}, bf16[6,32,512]{2,1,0:T(8,128)(2,1)S(1)}, bf16[6,32,512]{2,1,0:T(8,128)(2,1)S(1)}, f32[40,512]{1,0:T(8,128)S(1)}) custom-call(bf16[16,32,512]{2,1,0:T(8,128)(2,1)} %bitcast.44, f32[1,512]{1,0:T(1,128)} %scale1.1, f32[1,512]{1,0:T(1,128)} %shift1.1, f32[1,512]{1,0:T(1,128)} %scale2.1, ...), custom_call_target="tpu_custom_call" | custom-call | flops 72477573120 | tf_op jit(solution)/shard_map/prepare/pallas_call | solution.py:241
  1.3 0.1 collective-permute-start.52
  1.4 2.7 %collective-permute-start.51 = (bf16[6,32,512]{2,1,0:T(8,128)(2,1)S(1)}, bf16[6,32,512]{2,1,0:T(8,128)(2,1)S(1)}, u32[]{:S(2)}, u32[]{:S(2)}) collective-permute-start(bf16[6,32,512]{2,1,0:T(8,128)(2,1)S(1)} %get-tuple-element.570), channel_id=1, source_target_pairs={{0,8},{1,2},{2,1},{3,4},{4,3},{5,6},{6,5},{7,15},{8,0},{9,10},{10,... | collective-permute-start | bytes 589832 | tf_op jit(solution)/shard_map/ppermute | solution.py:319
  4.1 0.0 collective-permute-done.52.near
  4.1 0.0 copy-done
  4.1 0.0 copy-start.1
  4.1 3.4 %first.1 = (bf16[18,32,512]{2,1,0:T(8,128)(2,1)S(1)}, f32[18,32,512]{2,1,0:T(8,128)S(1)}) custom-call(bf16[16,32,512]{2,1,0:T(8,128)(2,1)S(1)} %get-tuple-element.569.image, bf16[6,32,512]{2,1,0:T(8,128)(2,1)S(1)} %collective-permute-done.52.near, bf16[3,1536,512]{2,1,0:T(8,128)(2,1)S(1)} %bitcast.23, f32[40,512]{1,0:T(8,128)S(1)} %get-tuple-element.572.vectors), custom_call_target="tpu_custom_call" | custom-call | flops 2717908992 | tf_op jit(solution)/shard_map/first/pallas_call | solution.py:241
  7.5 0.2 collective-permute-done.51.far
  7.7 0.0 copy-done.1
  7.7 4.6 %second.1 = (bf16[6,32,512]{2,1,0:T(8,128)(2,1)S(1)}, f32[6,32,512]{2,1,0:T(8,128)S(1)}, f32[6,32,512]{2,1,0:T(8,128)S(1)}, bf16[10,32,512]{2,1,0:T(8,128)(2,1)S...) custom-call(bf16[16,32,512]{2,1,0:T(8,128)(2,1)S(1)} %get-tuple-element.569.image, ...), custom_call_target="tpu_custom_call" | custom-call | flops 3321888768 | tf_op jit(solution)/shard_map/second/pallas_call | solution.py:241
  12.3 7.8 %conditional.1 = (bf16[22,32,512]{2,1,0:T(8,128)(2,1)S(1)}, bf16[6,32,512]{2,1,0:T(8,128)(2,1)S(1)}, bf16[3,1536,512]{2,1,0:T(8,128)(2,1)S(1)}, bf16[3,1536,512]{2,1,0:T(8,128)(2,1)S(1)}, f32[20,32,512]{2,1,0:T(8,128)S(1)}) conditional(s32[]{:T(128)} %bitcast.1, (bf16[10,32,512]{2,1,0:T(8,128)(2,1)S(1)}, ...), branch_computations={%region_0.0_spmd, %region_1.0_spmd, %region_2.0_spmd, %region_3.0_... | conditional | bytes 2883744 | solution.py:401
  12.3 0.5 %collective-permute-start.46 = (bf16[6,32,512]{2,1,0:T(8,128)(2,1)S(1)}, bf16[6,32,512]{2,1,0:T(8,128)(2,1)S(1)}, u32[]{:S(2)}, u32[]{:S(2)}) collective-permute-start(bf16[6,32,512]{2,1,0:T(8,128)(2,1)S(1)} %get-tuple-element.526), channel_id=1, source_target_pairs={{0,1},{1,0},{2,3},{3,2},{4,5},{5,4},{6,7},{7,6},{8,16},{9,17},{10,... | collective-permute-start | bytes 589832 | tf_op jit(solution)/shard_map/cond/branch_15_fun/ppermute | solution.py:381
  12.8 0.1 collective-permute-start.45
  12.9 1.0 %collective-permute-done.46.partner = bf16[6,32,512]{2,1,0:T(8,128)(2,1)S(1)} collective-permute-done((bf16[6,32,512]{2,1,0:T(8,128)(2,1)S(1)}, bf16[6,32,512]{2,1,0:T(8,128)(2,1)S(1)}, u32[]{:S(2)}, u32[]{:S(2)}) %collective-permute-start.46) | collective-permute-done | bytes 196640 | tf_op jit(solution)/shard_map/cond/branch_15_fun/ppermute | solution.py:381
  13.9 0.1 grad_far.32
  14.0 1.6 %collective-permute-start.47 = (bf16[6,32,512]{2,1,0:T(8,128)(2,1)S(1)}, bf16[6,32,512]{2,1,0:T(8,128)(2,1)S(1)}, u32[]{:S(2)}, u32[]{:S(2)}) collective-permute-start(bf16[6,32,512]{2,1,0:T(8,128)(2,1)S(1)} %grad_far.32), channel_id=1, source_target_pairs={{0,8},{1,2},{2,1},{3,4},{4,3},{5,6},{6,5},{7,15},{8,0},{9,10},{10,... | collective-permute-start | bytes 589832 | tf_op jit(solution)/shard_map/cond/branch_15_fun/ppermute | solution.py:319
  15.5 4.1 %bring.32 = (bf16[3,1536,512]{2,1,0:T(8,128)(2,1)S(1)}, bf16[3,1536,512]{2,1,0:T(8,128)(2,1)S(1)}, f32[20,32,512]{2,1,0:T(8,128)S(1)}) custom-call(bf16[3,1536,512]{2,1,0:T(8,128)(2,1)} %get-tuple-element.529.kernel2, bf16[3,1536,512]{2,1,0:T(8,128)(2,1)} %get-tuple-element.530.kernel1, f32[20,32,512]{2,1,0:T(8,128)} %get-tuple-element.531.fold), custom_call_target="tpu_custom_call" | custom-call | tf_op jit(solution)/shard_map/cond/branch_15_fun/bring/pallas_call | solution.py:241
  19.7 0.0 collective-permute-done.45.partner
  19.7 0.0 collective-permute-done.47.far
  19.7 0.2 grad_rest.32
  20.0 10.7 %collective-permute-start.53 = (bf16[6,32,512]{2,1,0:T(8,128)(2,1)S(1)}, bf16[6,32,512]{2,1,0:T(8,128)(2,1)S(1)}, u32[]{:S(2)}, u32[]{:S(2)}) collective-permute-start(bf16[6,32,512]{2,1,0:T(8,128)(2,1)S(1)} %get-tuple-element.582), channel_id=1, source_target_pairs={{0,1},{1,0},{2,3},{3,2},{4,5},{5,4},{6,7},{7,6},{8,9},{9,8},{10,11... | collective-permute-start | bytes 589832 | tf_op jit(solution)/shard_map/ppermute | solution.py:316
  30.7 1.1 %collective-permute-done.53.near = bf16[6,32,512]{2,1,0:T(8,128)(2,1)S(1)} collective-permute-done((bf16[6,32,512]{2,1,0:T(8,128)(2,1)S(1)}, bf16[6,32,512]{2,1,0:T(8,128)(2,1)S(1)}, u32[]{:S(2)}, u32[]{:S(2)}) %collective-permute-start.53) | collective-permute-done | bytes 196640 | tf_op jit(solution)/shard_map/ppermute | solution.py:316
  31.8 6.8 %backward.1 = bf16[16,32,512]{2,1,0:T(8,128)(2,1)} custom-call(bf16[6,32,512]{2,1,0:T(8,128)(2,1)S(1)} %collective-permute-done.53.near, bf16[22,32,512]{2,1,0:T(8,128)(2,1)S(1)} %get-tuple-element.583.grads, f32[20,32,512]{2,1,0:T(8,128)S(1)} %get-tuple-element.584.fold, bf16[3,1536,512]{2,1,0:T(8,128)(2,1)S(1)} %get-tuple-element.585.kernel2, ...), custom_call_target="tpu_custom_call" | custom-call | flops 5435817984 | tf_op jit(solution)/shard_map/backward/pallas_call | solution.py:241
Async XLA Ops:
  0.0 4.1 %copy-start = (bf16[1,3,3,512,512]{4,3,2,1,0:T(8,128)(2,1)S(1)}, bf16[1,3,3,512,512]{4,3,2,1,0:T(8,128)(2,1)}, u32[]{:S(2)}) copy-start(bf16[1,3,3,512,512]{4,3,2,1,0:T(8,128)(2,1)} %param.29) | copy-start | bytes 14155780
  1.3 2.8 %collective-permute-start.52 = (bf16[6,32,512]{2,1,0:T(8,128)(2,1)S(1)}, bf16[6,32,512]{2,1,0:T(8,128)(2,1)S(1)}, u32[]{:S(2)}, u32[]{:S(2)}) collective-permute-start(bf16[6,32,512]{2,1,0:T(8,128)(2,1)S(1)} %get-tuple-element.571), channel_id=1, source_target_pairs={{0,1},{1,0},{2,3},{3,2},{4,5},{5,4},{6,7},{7,6},{8,9},{9,8},{10,11... | collective-permute-start | bytes 589832 | tf_op jit(solution)/shard_map/ppermute | solution.py:316
  1.4 6.3 %collective-permute-start.51 = (bf16[6,32,512]{2,1,0:T(8,128)(2,1)S(1)}, bf16[6,32,512]{2,1,0:T(8,128)(2,1)S(1)}, u32[]{:S(2)}, u32[]{:S(2)}) collective-permute-start(bf16[6,32,512]{2,1,0:T(8,128)(2,1)S(1)} %get-tuple-element.570), channel_id=1, source_target_pairs={{0,8},{1,2},{2,1},{3,4},{4,3},{5,6},{6,5},{7,15},{8,0},{9,10},{10,... | collective-permute-start | bytes 589832 | tf_op jit(solution)/shard_map/ppermute | solution.py:319
  4.1 3.6 %copy-start.1 = (bf16[1,3,3,512,512]{4,3,2,1,0:T(8,128)(2,1)S(1)}, bf16[1,3,3,512,512]{4,3,2,1,0:T(8,128)(2,1)}, u32[]{:S(2)}) copy-start(bf16[1,3,3,512,512]{4,3,2,1,0:T(8,128)(2,1)} %param.32) | copy-start | bytes 14155780
  12.3 1.6 %collective-permute-start.46 = (bf16[6,32,512]{2,1,0:T(8,128)(2,1)S(1)}, bf16[6,32,512]{2,1,0:T(8,128)(2,1)S(1)}, u32[]{:S(2)}, u32[]{:S(2)}) collective-permute-start(bf16[6,32,512]{2,1,0:T(8,128)(2,1)S(1)} %get-tuple-element.526), channel_id=1, source_target_pairs={{0,1},{1,0},{2,3},{3,2},{4,5},{5,4},{6,7},{7,6},{8,16},{9,17},{10,... | collective-permute-start | bytes 589832 | tf_op jit(solution)/shard_map/cond/branch_15_fun/ppermute | solution.py:381
  12.8 6.8 %collective-permute-start.45 = (bf16[10,32,512]{2,1,0:T(8,128)(2,1)S(1)}, bf16[10,32,512]{2,1,0:T(8,128)(2,1)S(1)}, u32[]{:S(2)}, u32[]{:S(2)}) collective-permute-start(bf16[10,32,512]{2,1,0:T(8,128)(2,1)S(1)} %get-tuple-element.523), channel_id=1, source_target_pairs={{0,1},{1,0},{2,3},{3,2},{4,5},{5,4},{6,7},{7,6},{8,16},{9,17},{10,... | collective-permute-start | bytes 983048 | tf_op jit(solution)/shard_map/cond/branch_15_fun/ppermute | solution.py:382
  14.0 5.7 %collective-permute-start.47 = (bf16[6,32,512]{2,1,0:T(8,128)(2,1)S(1)}, bf16[6,32,512]{2,1,0:T(8,128)(2,1)S(1)}, u32[]{:S(2)}, u32[]{:S(2)}) collective-permute-start(bf16[6,32,512]{2,1,0:T(8,128)(2,1)S(1)} %grad_far.32), channel_id=1, source_target_pairs={{0,8},{1,2},{2,1},{3,4},{4,3},{5,6},{6,5},{7,15},{8,0},{9,10},{10,... | collective-permute-start | bytes 589832 | tf_op jit(solution)/shard_map/cond/branch_15_fun/ppermute | solution.py:319
  20.0 11.8 %collective-permute-start.53 = (bf16[6,32,512]{2,1,0:T(8,128)(2,1)S(1)}, bf16[6,32,512]{2,1,0:T(8,128)(2,1)S(1)}, u32[]{:S(2)}, u32[]{:S(2)}) collective-permute-start(bf16[6,32,512]{2,1,0:T(8,128)(2,1)S(1)} %get-tuple-element.582), channel_id=1, source_target_pairs={{0,1},{1,0},{2,3},{3,2},{4,5},{5,4},{6,7},{7,6},{8,9},{9,8},{10,11... | collective-permute-start | bytes 589832 | tf_op jit(solution)/shard_map/ppermute | solution.py:316
where the time goes:
time: 38.4 us; the launch traced here: 38.6 us
  Pallas kernels  20.3 us (53%)
  starting transfers between devices  15.7 us (41%)
  waiting for transfers between devices  2.26 us (6%)
    pallas_call x7, Pallas kernels, call(): pl.pallas_call(body, out_shape=[o if i == result else k(o.shape, o.dtype)...  20.3 us
    ppermute x2, starting transfers between devices, near(): return lax.ppermute(rows, 'space', pairs)  10.8 us
    ppermute x2, starting transfers between devices, far(): return lax.ppermute(rows, ('peer', 'space'), across)  4.3 us
    ppermute x2, waiting for transfers between devices, near(): return lax.ppermute(rows, 'space', pairs)  1.07 us
    ppermute x1, waiting for transfers between devices, exchange(): partner_far = swap(feat_far)  1 us
  transfers between devices with their start and end apart: 6, of which 3 were waited for; matrix products, arithmetic and copies ran while one was open for 0% of the time, Pallas kernels for 20%

commit v1 on v0

--- a/solution.py
+++ b/solution.py
@@ -147,23 +147,27 @@
 
 def second(
     image, far, hidden, slope, kernel1, kernel2, vectors, task,
-    feat_far, base_far, rate_far, feat_near, base_near, rate_near, fold,
-    cat1, cat2, rim, slope1, slope2, part, feat, sems
+    task_far, feat_far, slope_far, task_near, feat_near, slope_near, fold,
+    cat1, cat2, rim, slope1, slope2, feat, sems
 ):
     odd = side()
     strip, edge, held = image.shape[0], far.shape[0], hidden.shape[0]
     most = held - D1
+    far_at = pl.ds(pick(odd, 0, strip - edge), edge)
+    near_at = pl.ds(pick(odd, edge, 0), strip - edge)
     copies = [
-        pltpu.make_async_copy(task, part, sems.at[0]),
+        pltpu.make_async_copy(task.at[far_at], task_far, sems.at[0]),
         pltpu.make_async_copy(
             slope.at[pl.ds(pick(odd, 0, D1), most)], fold.at[pl.ds(pick(odd, D2, 0), most)], sems.at[1]
         ),
         pltpu.make_async_copy(
             slope1.at[pl.ds(pick(odd, D1, 0), D2)], fold.at[pl.ds(pick(odd, 0, most), D2)], sems.at[2]
         ),
+        pltpu.make_async_copy(task.at[near_at], task_near, sems.at[3]),
     ]
     copies[0].start()
     copies[1].start()
+    copies[3].start()
     own = 2 * D1
     put_far(cat1, pick(odd, 0, own), far, D1)
     put(cat1, pick(odd, edge, 0), own, image[pl.ds(pick(odd, 0, strip - own), own)], D1)
@@ -175,27 +179,30 @@
     conv_act(cat2, kernel2, vectors[16:17], vectors[24:25], D2, feat, slope2)
     for copy in copies:
         copy.wait()
+    for at, part, rate in ((far_at, feat_far, slope_far), (near_at, feat_near, slope_near)):
+        part[...] = feat[at]
+        rate[...] = slope2[at]
+
+
+def gradient(task, feat, slope, partner, vectors, grad):
     paired = vectors[32:33]
-    far_at = pl.ds(pick(odd, 0, strip - edge), edge)
-    near_at = pl.ds(pick(odd, edge, 0), strip - edge)
-    for at, own, base, rate in ((far_at, feat_far, base_far, rate_far), (near_at, feat_near, base_near, rate_near)):
-        own[...] = feat[at]
-        rate[...] = slope2[at] * paired
-        base[...] = (part[at].astype(F32) + feat[at].astype(F32) * paired) * slope2[at]
-
-
-def gradient(base, rate, partner, grad):
+
     def step(row, carry):
-        grad[row] = (base[row] - partner[row].astype(F32) * rate[row]).astype(BF16)
+        apart = (feat[row].astype(F32) - partner[row].astype(F32)) * paired
+        grad[row] = ((task[row].astype(F32) + apart) * slope[row]).astype(BF16)
         return carry
 
     lax.fori_loop(0, grad.shape[0], step, 0, unroll=2)
 
 
-def grad_rest(base, rate, partner, grad_far, far, grads, near_send):
+def grad_first(task, feat, slope, partner, vectors, mark, grad):
+    gradient(task, feat, slope, partner, vectors, grad)
+
+
+def grad_rest(task, feat, slope, partner, vectors, grad_far, far, grads, near_send):
     odd = side()
     rows, edge = partner.shape[0], grad_far.shape[0]
-    gradient(base, rate, partner, grads.at[pl.ds(pick(odd, 2 * edge, 0), rows)])
+    gradient(task, feat, slope, partner, vectors, grads.at[pl.ds(pick(odd, 2 * edge, 0), rows)])
     grads[pl.ds(pick(odd, edge, rows), edge)] = grad_far[...]
     beyond = pl.ds(pick(odd, 0, edge + rows), edge)
     grads[beyond] = far[...]
@@ -207,11 +214,12 @@
     near_send[...] = grads[pl.ds(pick(odd, edge + rows, 0), edge)]
 
 
-def bring(kernel2, kernel1, fold, kept2, kept1, slope, sems):
+def bring(kernel2, kernel1, fold, kept2, kept1, slope, mark, sems):
     pairs = ((kernel2, kept2), (kernel1, kept1), (fold, slope))
     copies = [pltpu.make_async_copy(source, target, sems.at[i]) for i, (source, target) in enumerate(pairs)]
     for copy in copies:
         copy.start()
+    mark[...] = jnp.zeros_like(mark)
     for copy in copies:
         copy.wait()
 
@@ -303,6 +311,7 @@
     space, groups = lax.axis_size("space"), lax.axis_size("peer")
     pairs = [(i, i ^ 1) for i in range(space)]
     across = [(p * space + i, far_side(p, i, groups, space)) for p in range(groups) for i in range(space)]
+    inside = [(p * space + i, p * space + (i + 1 if i % 2 else i - 1)) for p in range(groups) for i in range(1, space - 1)]
     per_row = 2 * 9 * width * chans * chans
     deep = strip + EDGE - 2 * D1
 
@@ -315,8 +324,8 @@
     def near(rows):
         return lax.ppermute(rows, "space", pairs)
 
-    def far(rows):
-        return lax.ppermute(rows, ("peer", "space"), across)
+    def far(rows, pairs):
+        return lax.ppermute(rows, ("peer", "space"), pairs)
 
     routed = math.factorial(groups) <= MAX_ROUTES
     routes, chosen = routes_of(groups) if routed else ((), ())
@@ -337,7 +346,7 @@
         remote=range(6),
     )
     near_halo = near(near_send)
-    far_halo = far(far_send)
+    far_halo = far(far_send, across)
     hidden, slope1 = call(
         first,
         "first",
@@ -353,10 +362,10 @@
         (image, far_halo, hidden, slope1, kernel1, kernel2, vectors, task),
         (
             rows_of(EDGE),
-            rows_of(EDGE, F32),
+            rows_of(EDGE),
             rows_of(EDGE, F32),
             rows_of(inner),
-            rows_of(inner, F32),
+            rows_of(inner),
             rows_of(inner, F32),
             rows_of(strip + 2 * D1, F32),
         ),
@@ -367,8 +376,7 @@
             rows_of(EDGE, F32),
             rows_of(strip, F32),
             rows_of(strip),
-            rows_of(strip),
-            dma((3,)),
+            dma((4,)),
         ),
         flops=per_row * (EDGE + strip),
         remote=(7,),
@@ -377,19 +385,29 @@
 
     whole = jax.ShapeDtypeStruct(kernel1.shape, BF16)
 
-    def exchange(swap, feat_far, base_far, rate_far, feat_near, base_near, rate_near, *stored):
+    def exchange(swap, task_far, feat_far, slope_far, task_near, feat_near, slope_near, vectors, *stored):
         partner_far = swap(feat_far)
         partner_near = swap(feat_near)
-        (grad_far,) = call(gradient, "grad_far", (base_far, rate_far, partner_far), (rows_of(EDGE),))
-        far_grad = far(grad_far)
+        *brought, mark = call(
+            bring,
+            "bring",
+            stored,
+            (whole, whole, rows_of(strip + 2 * D1, F32), jax.ShapeDtypeStruct((8, 128), F32)),
+            (dma((3,)),),
+            remote=range(3),
+        )
+        (grad_far,) = call(
+            grad_first,
+            "grad_first",
+            (task_far, feat_far, slope_far, partner_far, vectors, mark),
+            (rows_of(EDGE),),
+        )
+        far_grad = far(grad_far, inside)
         grads, near_send = call(
             grad_rest,
             "grad_rest",
-            (base_near, rate_near, partner_near, grad_far, far_grad),
+            (task_near, feat_near, slope_near, partner_near, vectors, grad_far, far_grad),
             (rows_of(strip + EDGE), rows_of(EDGE)),
-        )
-        brought = call(
-            bring, "bring", stored, (whole, whole, rows_of(strip + 2 * D1, F32)), (dma((3,)),), remote=range(3)
         )
         return grads, near_send, *brought
 
@@ -398,9 +416,9 @@
             functools.partial(lax.ppermute, axis_name=("peer", "space"), perm=spread(route, groups, space))
             for route in routes
         ]
-        state = lax.switch(index[0], [functools.partial(exchange, move) for move in moves], *given, kernel2, kernel1, fold)
+        state = lax.switch(index[0], [functools.partial(exchange, move) for move in moves], *given, vectors, kernel2, kernel1, fold)
     else:
-        state = exchange(functools.partial(swap_blocks, pairing=pairing), *given, kernel2, kernel1, fold)
+        state = exchange(functools.partial(swap_blocks, pairing=pairing), *given, vectors, kernel2, kernel1, fold)
     grads, near_send, kernel2, kernel1, fold = state
     near_grad = near(near_send)
     back = strip + 2 * D1

time: 38.4 us -> 36.4 us (0.948)
  the two profiles are of different devices: /device:TPU:1 before, /device:TPU:0 now
where the time goes in v1:
time: 36.4 us; the launch traced here: 35.7 us
  Pallas kernels  20.4 us (56%)
  starting transfers between devices  7.63 us (21%)
  waiting for transfers between devices  7.44 us (20%)
    pallas_call x7, Pallas kernels, call(): pl.pallas_call(body, out_shape=[o if i == result else k(o.shape, o.dtype)...  20.4 us
    ppermute x1, waiting for transfers between devices, exchange(): partner_near = swap(feat_near)  5.34 us
    ppermute x2, starting transfers between devices, far(): return lax.ppermute(rows, ('peer', 'space'), pairs)  3.24 us
    ppermute x1, starting transfers between devices, exchange(): partner_far = swap(feat_far)  3.03 us
    ppermute x2, waiting for transfers between devices, near(): return lax.ppermute(rows, 'space', pairs)  1.17 us
    ppermute x2, starting transfers between devices, near(): return lax.ppermute(rows, 'space', pairs)  0.86 us
  transfers between devices with their start and end apart: 6, of which 4 were waited for; matrix products, arithmetic and copies ran while one was open for 0% of the time, Pallas kernels for 21%

profile of v1, /device:TPU:0, one launch (start us, length us, event | category | flops | bytes accessed | tf_op | source)
XLA Modules:
  0.0 35.7 jit_solution(14377163334942168183)
XLA Ops:
  0.0 0.0 copy-start
  0.0 1.3 %prepare.1 = (s32[1]{0:T(128)S(4)}, bf16[16,32,512]{2,1,0:T(8,128)(2,1)S(1)}, bf16[6,32,512]{2,1,0:T(8,128)(2,1)S(1)}, bf16[6,32,512]{2,1,0:T(8,128)(2,1)S(1)}, f32[40,512]{1,0:T(8,128)S(1)}) custom-call(bf16[16,32,512]{2,1,0:T(8,128)(2,1)} %bitcast.44, f32[1,512]{1,0:T(1,128)} %scale1.1, f32[1,512]{1,0:T(1,128)} %shift1.1, f32[1,512]{1,0:T(1,128)} %scale2.1, ...), custom_call_target="tpu_custom_call" | custom-call | flops 72477573120 | tf_op jit(solution)/shard_map/prepare/pallas_call | solution.py:249
  1.3 0.5 %collective-permute-start.52 = (bf16[6,32,512]{2,1,0:T(8,128)(2,1)S(1)}, bf16[6,32,512]{2,1,0:T(8,128)(2,1)S(1)}, u32[]{:S(2)}, u32[]{:S(2)}) collective-permute-start(bf16[6,32,512]{2,1,0:T(8,128)(2,1)S(1)} %get-tuple-element.639), channel_id=1, source_target_pairs={{0,1},{1,0},{2,3},{3,2},{4,5},{5,4},{6,7},{7,6},{8,9},{9,8},{10,11... | collective-permute-start | bytes 589832 | tf_op jit(solution)/shard_map/ppermute | solution.py:325
  1.8 2.6 %collective-permute-start.51 = (bf16[6,32,512]{2,1,0:T(8,128)(2,1)S(1)}, bf16[6,32,512]{2,1,0:T(8,128)(2,1)S(1)}, u32[]{:S(2)}, u32[]{:S(2)}) collective-permute-start(bf16[6,32,512]{2,1,0:T(8,128)(2,1)S(1)} %get-tuple-element.638), channel_id=1, source_target_pairs={{0,8},{1,2},{2,1},{3,4},{4,3},{5,6},{6,5},{7,15},{8,0},{9,10},{10,... | collective-permute-start | bytes 589832 | tf_op jit(solution)/shard_map/ppermute | solution.py:328
  4.4 0.0 collective-permute-done.52.near
  4.4 0.0 copy-done
  4.4 0.0 copy-start.1
  4.4 3.4 %first.1 = (bf16[18,32,512]{2,1,0:T(8,128)(2,1)S(1)}, f32[18,32,512]{2,1,0:T(8,128)S(1)}) custom-call(bf16[16,32,512]{2,1,0:T(8,128)(2,1)S(1)} %get-tuple-element.637.image, bf16[6,32,512]{2,1,0:T(8,128)(2,1)S(1)} %collective-permute-done.52.near, bf16[3,1536,512]{2,1,0:T(8,128)(2,1)S(1)} %bitcast.23, f32[40,512]{1,0:T(8,128)S(1)} %get-tuple-element.640.vectors), custom_call_target="tpu_custom_call" | custom-call | flops 2717908992 | tf_op jit(solution)/shard_map/first/pallas_call | solution.py:249
  7.7 0.3 collective-permute-done.51.far
  8.0 0.0 copy-done.1
  8.0 4.5 %second.1 = (bf16[6,32,512]{2,1,0:T(8,128)(2,1)S(1)}, bf16[6,32,512]{2,1,0:T(8,128)(2,1)S(1)}, f32[6,32,512]{2,1,0:T(8,128)S(1)}, bf16[10,32,512]{2,1,0:T(8,128)...) custom-call(bf16[16,32,512]{2,1,0:T(8,128)(2,1)S(1)} %get-tuple-element.637.image, ...), custom_call_target="tpu_custom_call" | custom-call | flops 3321888768 | tf_op jit(solution)/shard_map/second/pallas_call | solution.py:249
  12.5 14.9 %conditional.1 = (bf16[22,32,512]{2,1,0:T(8,128)(2,1)S(1)}, bf16[6,32,512]{2,1,0:T(8,128)(2,1)S(1)}, bf16[3,1536,512]{2,1,0:T(8,128)(2,1)S(1)}, bf16[3,1536,512]{2,1,0:T(8,128)(2,1)S(1)}, f32[20,32,512]{2,1,0:T(8,128)S(1)}) conditional(s32[]{:T(128)} %bitcast.1, (bf16[10,32,512]{2,1,0:T(8,128)(2,1)S(1)}, ...), branch_computations={%region_0.0_spmd, %region_1.0_spmd, %region_2.0_spmd, %region_3.0_... | conditional | bytes 2883744 | solution.py:419
  12.6 3.0 %collective-permute-start.22 = (bf16[6,32,512]{2,1,0:T(8,128)(2,1)S(1)}, bf16[6,32,512]{2,1,0:T(8,128)(2,1)S(1)}, u32[]{:S(2)}, u32[]{:S(2)}) collective-permute-start(bf16[6,32,512]{2,1,0:T(8,128)(2,1)S(1)} %get-tuple-element.462.feat), channel_id=1, source_target_pairs={{0,24},{1,25},{2,26},{3,27},{4,28},{5,29},{6,30},{7,31},{8,16},{9,... | collective-permute-start | bytes 589832 | tf_op jit(solution)/shard_map/cond/branch_7_fun/ppermute | solution.py:389
  15.6 0.5 %collective-permute-start.21 = (bf16[10,32,512]{2,1,0:T(8,128)(2,1)S(1)}, bf16[10,32,512]{2,1,0:T(8,128)(2,1)S(1)}, u32[]{:S(2)}, u32[]{:S(2)}) collective-permute-start(bf16[10,32,512]{2,1,0:T(8,128)(2,1)S(1)} %get-tuple-element.458.feat), channel_id=1, source_target_pairs={{0,24},{1,25},{2,26},{3,27},{4,28},{5,29},{6,30},{7,31},{8,16},{9,... | collective-permute-start | bytes 983048 | tf_op jit(solution)/shard_map/cond/branch_7_fun/ppermute | solution.py:390
  16.1 4.1 %bring.24 = (bf16[3,1536,512]{2,1,0:T(8,128)(2,1)S(1)}, bf16[3,1536,512]{2,1,0:T(8,128)(2,1)S(1)}, f32[20,32,512]{2,1,0:T(8,128)S(1)}, f32[8,128]{1,0:T(8,128)S(1)}) custom-call(bf16[3,1536,512]{2,1,0:T(8,128)(2,1)} %get-tuple-element.464.kernel2, bf16[3,1536,512]{2,1,0:T(8,128)(2,1)} %get-tuple-element.465.kernel1, f32[20,32,512]{2,1,0:T(8,128)} %get-tuple-element.466.fold), custom_call_target="tpu_custom_call" | custom-call | tf_op jit(solution)/shard_map/cond/branch_7_fun/bring/pallas_call | solution.py:249
  20.2 0.6 %collective-permute-done.22.partner = bf16[6,32,512]{2,1,0:T(8,128)(2,1)S(1)} collective-permute-done((bf16[6,32,512]{2,1,0:T(8,128)(2,1)S(1)}, bf16[6,32,512]{2,1,0:T(8,128)(2,1)S(1)}, u32[]{:S(2)}, u32[]{:S(2)}) %collective-permute-start.22) | collective-permute-done | bytes 196640 | tf_op jit(solution)/shard_map/cond/branch_7_fun/ppermute | solution.py:389
  20.9 0.1 grad_first.24.grad_far
  21.0 0.7 %collective-permute-start.23 = (bf16[6,32,512]{2,1,0:T(8,128)(2,1)S(1)}, bf16[6,32,512]{2,1,0:T(8,128)(2,1)S(1)}, u32[]{:S(2)}, u32[]{:S(2)}) collective-permute-start(bf16[6,32,512]{2,1,0:T(8,128)(2,1)S(1)} %grad_first.24.grad_far), channel_id=1, source_target_pairs={{1,2},{2,1},{3,4},{4,3},{5,6},{6,5},{9,10},{10,9},{11,12},{12,11},... | collective-permute-start | bytes 589832 | tf_op jit(solution)/shard_map/cond/branch_7_fun/ppermute | solution.py:328
  21.7 5.3 %collective-permute-done.21.partner = bf16[10,32,512]{2,1,0:T(8,128)(2,1)S(1)} collective-permute-done((bf16[10,32,512]{2,1,0:T(8,128)(2,1)S(1)}, bf16[10,32,512]{2,1,0:T(8,128)(2,1)S(1)}, u32[]{:S(2)}, u32[]{:S(2)}) %collective-permute-start.21) | collective-permute-done | bytes 327712 | tf_op jit(solution)/shard_map/cond/branch_7_fun/ppermute | solution.py:390
  27.0 0.0 collective-permute-done.23.far
  27.0 0.2 grad_rest.24
  27.5 0.3 collective-permute-start.53
  27.8 1.2 %collective-permute-done.53.near = bf16[6,32,512]{2,1,0:T(8,128)(2,1)S(1)} collective-permute-done((bf16[6,32,512]{2,1,0:T(8,128)(2,1)S(1)}, bf16[6,32,512]{2,1,0:T(8,128)(2,1)S(1)}, u32[]{:S(2)}, u32[]{:S(2)}) %collective-permute-start.53) | collective-permute-done | bytes 196640 | tf_op jit(solution)/shard_map/ppermute | solution.py:325
  29.0 6.8 %backward.1 = bf16[16,32,512]{2,1,0:T(8,128)(2,1)} custom-call(bf16[6,32,512]{2,1,0:T(8,128)(2,1)S(1)} %collective-permute-done.53.near, bf16[22,32,512]{2,1,0:T(8,128)(2,1)S(1)} %get-tuple-element.651.grads, f32[20,32,512]{2,1,0:T(8,128)S(1)} %get-tuple-element.652.fold, bf16[3,1536,512]{2,1,0:T(8,128)(2,1)S(1)} %get-tuple-element.653.kernel2, ...), custom_call_target="tpu_custom_call" | custom-call | flops 5435817984 | tf_op jit(solution)/shard_map/backward/pallas_call | solution.py:249
Async XLA Ops:
  0.0 4.4 %copy-start = (bf16[1,3,3,512,512]{4,3,2,1,0:T(8,128)(2,1)S(1)}, bf16[1,3,3,512,512]{4,3,2,1,0:T(8,128)(2,1)}, u32[]{:S(2)}) copy-start(bf16[1,3,3,512,512]{4,3,2,1,0:T(8,128)(2,1)} %param.29) | copy-start | bytes 14155780
  1.3 3.1 %collective-permute-start.52 = (bf16[6,32,512]{2,1,0:T(8,128)(2,1)S(1)}, bf16[6,32,512]{2,1,0:T(8,128)(2,1)S(1)}, u32[]{:S(2)}, u32[]{:S(2)}) collective-permute-start(bf16[6,32,512]{2,1,0:T(8,128)(2,1)S(1)} %get-tuple-element.639), channel_id=1, source_target_pairs={{0,1},{1,0},{2,3},{3,2},{4,5},{5,4},{6,7},{7,6},{8,9},{9,8},{10,11... | collective-permute-start | bytes 589832 | tf_op jit(solution)/shard_map/ppermute | solution.py:325
  1.8 6.2 %collective-permute-start.51 = (bf16[6,32,512]{2,1,0:T(8,128)(2,1)S(1)}, bf16[6,32,512]{2,1,0:T(8,128)(2,1)S(1)}, u32[]{:S(2)}, u32[]{:S(2)}) collective-permute-start(bf16[6,32,512]{2,1,0:T(8,128)(2,1)S(1)} %get-tuple-element.638), channel_id=1, source_target_pairs={{0,8},{1,2},{2,1},{3,4},{4,3},{5,6},{6,5},{7,15},{8,0},{9,10},{10,... | collective-permute-start | bytes 589832 | tf_op jit(solution)/shard_map/ppermute | solution.py:328
  4.4 3.6 %copy-start.1 = (bf16[1,3,3,512,512]{4,3,2,1,0:T(8,128)(2,1)S(1)}, bf16[1,3,3,512,512]{4,3,2,1,0:T(8,128)(2,1)}, u32[]{:S(2)}) copy-start(bf16[1,3,3,512,512]{4,3,2,1,0:T(8,128)(2,1)} %param.32) | copy-start | bytes 14155780
  12.6 8.3 %collective-permute-start.22 = (bf16[6,32,512]{2,1,0:T(8,128)(2,1)S(1)}, bf16[6,32,512]{2,1,0:T(8,128)(2,1)S(1)}, u32[]{:S(2)}, u32[]{:S(2)}) collective-permute-start(bf16[6,32,512]{2,1,0:T(8,128)(2,1)S(1)} %get-tuple-element.462.feat), channel_id=1, source_target_pairs={{0,24},{1,25},{2,26},{3,27},{4,28},{5,29},{6,30},{7,31},{8,16},{9,... | collective-permute-start | bytes 589832 | tf_op jit(solution)/shard_map/cond/branch_7_fun/ppermute | solution.py:389
  15.6 11.4 %collective-permute-start.21 = (bf16[10,32,512]{2,1,0:T(8,128)(2,1)S(1)}, bf16[10,32,512]{2,1,0:T(8,128)(2,1)S(1)}, u32[]{:S(2)}, u32[]{:S(2)}) collective-permute-start(bf16[10,32,512]{2,1,0:T(8,128)(2,1)S(1)} %get-tuple-element.458.feat), channel_id=1, source_target_pairs={{0,24},{1,25},{2,26},{3,27},{4,28},{5,29},{6,30},{7,31},{8,16},{9,... | collective-permute-start | bytes 983048 | tf_op jit(solution)/shard_map/cond/branch_7_fun/ppermute | solution.py:390
  21.0 6.0 %collective-permute-start.23 = (bf16[6,32,512]{2,1,0:T(8,128)(2,1)S(1)}, bf16[6,32,512]{2,1,0:T(8,128)(2,1)S(1)}, u32[]{:S(2)}, u32[]{:S(2)}) collective-permute-start(bf16[6,32,512]{2,1,0:T(8,128)(2,1)S(1)} %grad_first.24.grad_far), channel_id=1, source_target_pairs={{1,2},{2,1},{3,4},{4,3},{5,6},{6,5},{9,10},{10,9},{11,12},{12,11},... | collective-permute-start | bytes 589832 | tf_op jit(solution)/shard_map/cond/branch_7_fun/ppermute | solution.py:328
  27.5 1.5 %collective-permute-start.53 = (bf16[6,32,512]{2,1,0:T(8,128)(2,1)S(1)}, bf16[6,32,512]{2,1,0:T(8,128)(2,1)S(1)}, u32[]{:S(2)}, u32[]{:S(2)}) collective-permute-start(bf16[6,32,512]{2,1,0:T(8,128)(2,1)S(1)} %get-tuple-element.650), channel_id=1, source_target_pairs={{0,1},{1,0},{2,3},{3,2},{4,5},{5,4},{6,7},{7,6},{8,9},{9,8},{10,11... | collective-permute-start | bytes 589832 | tf_op jit(solution)/shard_map/ppermute | solution.py:325

commit v2 on v1

--- a/solution.py
+++ b/solution.py
@@ -147,14 +147,15 @@
 
 def second(
     image, far, hidden, slope, kernel1, kernel2, vectors, task,
-    task_far, feat_far, slope_far, task_near, feat_near, slope_near, fold,
+    task_far, feat_far, slope_far, task_near, feat_near, slope_near, task_mid, feat_mid, slope_mid, fold,
     cat1, cat2, rim, slope1, slope2, feat, sems
 ):
     odd = side()
     strip, edge, held = image.shape[0], far.shape[0], hidden.shape[0]
     most = held - D1
     far_at = pl.ds(pick(odd, 0, strip - edge), edge)
-    near_at = pl.ds(pick(odd, edge, 0), strip - edge)
+    near_at = pl.ds(pick(odd, strip - edge, 0), edge)
+    mid_at = pl.ds(edge, strip - 2 * edge)
     copies = [
         pltpu.make_async_copy(task.at[far_at], task_far, sems.at[0]),
         pltpu.make_async_copy(
@@ -164,10 +165,10 @@
             slope1.at[pl.ds(pick(odd, D1, 0), D2)], fold.at[pl.ds(pick(odd, 0, most), D2)], sems.at[2]
         ),
         pltpu.make_async_copy(task.at[near_at], task_near, sems.at[3]),
+        pltpu.make_async_copy(task.at[mid_at], task_mid, sems.at[4]),
     ]
-    copies[0].start()
-    copies[1].start()
-    copies[3].start()
+    for i in (0, 1, 3, 4):
+        copies[i].start()
     own = 2 * D1
     put_far(cat1, pick(odd, 0, own), far, D1)
     put(cat1, pick(odd, edge, 0), own, image[pl.ds(pick(odd, 0, strip - own), own)], D1)
@@ -179,7 +180,8 @@
     conv_act(cat2, kernel2, vectors[16:17], vectors[24:25], D2, feat, slope2)
     for copy in copies:
         copy.wait()
-    for at, part, rate in ((far_at, feat_far, slope_far), (near_at, feat_near, slope_near)):
+    parts = ((far_at, feat_far, slope_far), (near_at, feat_near, slope_near), (mid_at, feat_mid, slope_mid))
+    for at, part, rate in parts:
         part[...] = feat[at]
         rate[...] = slope2[at]
 
@@ -199,19 +201,20 @@
     gradient(task, feat, slope, partner, vectors, grad)
 
 
-def grad_rest(task, feat, slope, partner, vectors, grad_far, far, grads, near_send):
+def gather(far, grad_far, grad_mid, grad_near, near, grads):
     odd = side()
-    rows, edge = partner.shape[0], grad_far.shape[0]
-    gradient(task, feat, slope, partner, vectors, grads.at[pl.ds(pick(odd, 2 * edge, 0), rows)])
-    grads[pl.ds(pick(odd, edge, rows), edge)] = grad_far[...]
-    beyond = pl.ds(pick(odd, 0, edge + rows), edge)
+    edge, mid = far.shape[0], grad_mid.shape[0]
+    beyond = pl.ds(pick(odd, 0, 3 * edge + mid), edge)
     grads[beyond] = far[...]
 
     @pl.when(at_end())
     def _():
         grads[beyond] = jnp.zeros(far.shape, far.dtype)
 
-    near_send[...] = grads[pl.ds(pick(odd, edge + rows, 0), edge)]
+    grads[pl.ds(pick(odd, edge, 2 * edge + mid), edge)] = grad_far[...]
+    grads[pl.ds(2 * edge, mid)] = grad_mid[...]
+    grads[pl.ds(pick(odd, 2 * edge + mid, edge), edge)] = grad_near[...]
+    grads[pl.ds(pick(odd, 3 * edge + mid, 0), edge)] = near[...]
 
 
 def bring(kernel2, kernel1, fold, kept2, kept1, slope, mark, sems):
@@ -224,16 +227,14 @@
         copy.wait()
 
 
-def backward(near, grads, fold, kernel2, kernel1, out, cat2, cat1, grad1):
-    odd = side()
-    edge, held, width, rows = near.shape[0], grads.shape[0], near.shape[1], grad1.shape[0]
-    put(cat2, pick(odd, held, 0), edge, near[...], D2)
-    put(cat2, pick(odd, 0, edge), held, grads[...], D2)
+def backward(grads, fold, kernel2, kernel1, out, cat2, cat1, grad1):
+    width, rows = grads.shape[1], grad1.shape[0]
+    put(cat2, 0, grads.shape[0], grads[...], D2)
     for lo, size in halves(grad1.shape[2]):
         cut = slice(lo, lo + size)
         back = conv_t(cat2, kernel2, D2, rows, lo, size).reshape(rows, width, size)
         grad1[:, :, cut] = (back * fold[:, :, cut]).astype(BF16)
-    hide_beyond(grad1, odd, D1)
+    hide_beyond(grad1, side(), D1)
     put(cat1, 0, rows, grad1[...], D1)
     rows = out.shape[0]
     for lo, size in halves(out.shape[2]):
@@ -355,18 +356,13 @@
         (cat_of(strip + EDGE),),
         flops=per_row * deep,
     )
-    inner = strip - EDGE
+    mid = strip - 2 * EDGE
     *given, fold = call(
         second,
         "second",
         (image, far_halo, hidden, slope1, kernel1, kernel2, vectors, task),
         (
-            rows_of(EDGE),
-            rows_of(EDGE),
-            rows_of(EDGE, F32),
-            rows_of(inner),
-            rows_of(inner),
-            rows_of(inner, F32),
+            *[rows_of(count, kind) for count in (EDGE, EDGE, mid) for kind in (BF16, BF16, F32)],
             rows_of(strip + 2 * D1, F32),
         ),
         (
@@ -376,18 +372,18 @@
             rows_of(EDGE, F32),
             rows_of(strip, F32),
             rows_of(strip),
-            dma((4,)),
+            dma((5,)),
         ),
         flops=per_row * (EDGE + strip),
         remote=(7,),
-        stored=(6,),
+        stored=(9,),
     )
 
     whole = jax.ShapeDtypeStruct(kernel1.shape, BF16)
 
-    def exchange(swap, task_far, feat_far, slope_far, task_near, feat_near, slope_near, vectors, *stored):
-        partner_far = swap(feat_far)
-        partner_near = swap(feat_near)
+    def exchange(swap, *given):
+        far_given, near_given, mid_given, (vectors, *stored) = given[:3], given[3:6], given[6:9], given[9:]
+        partner_far, partner_near, partner_mid = swap(far_given[1]), swap(near_given[1]), swap(mid_given[1])
         *brought, mark = call(
             bring,
             "bring",
@@ -399,17 +395,25 @@
         (grad_far,) = call(
             grad_first,
             "grad_first",
-            (task_far, feat_far, slope_far, partner_far, vectors, mark),
+            (*far_given, partner_far, vectors, mark),
             (rows_of(EDGE),),
+            flops=0 * per_row,
         )
         far_grad = far(grad_far, inside)
-        grads, near_send = call(
-            grad_rest,
-            "grad_rest",
-            (task_near, feat_near, slope_near, partner_near, vectors, grad_far, far_grad),
-            (rows_of(strip + EDGE), rows_of(EDGE)),
+        (grad_near,) = call(
+            grad_first,
+            "grad_near",
+            (*near_given, partner_near, vectors, grad_far),
+            (rows_of(EDGE),),
+            flops=0 * per_row,
         )
-        return grads, near_send, *brought
+        (grad_mid,) = call(
+            gradient, "grad_mid", (*mid_given, partner_mid, vectors), (rows_of(mid),), flops=18 * per_row
+        )
+        (grads,) = call(
+            gather, "gather", (far_grad, grad_far, grad_mid, grad_near, near(grad_near)), (rows_of(strip + 2 * EDGE),)
+        )
+        return grads, *brought
 
     if routed:
         moves = [
@@ -419,13 +423,12 @@
         state = lax.switch(index[0], [functools.partial(exchange, move) for move in moves], *given, vectors, kernel2, kernel1, fold)
     else:
         state = exchange(functools.partial(swap_blocks, pairing=pairing), *given, vectors, kernel2, kernel1, fold)
-    grads, near_send, kernel2, kernel1, fold = state
-    near_grad = near(near_send)
+    grads, kernel2, kernel1, fold = state
     back = strip + 2 * D1
     (out,) = call(
         backward,
         "backward",
-        (near_grad, grads, fold, kernel2, kernel1),
+        (grads, fold, kernel2, kernel1),
         (rows_of(strip),),
         (cat_of(strip + 2 * EDGE), cat_of(back), rows_of(back)),
         flops=per_row * (back + strip),

time: 36.4 us -> 34 us (0.934)
  the two profiles are of different devices: /device:TPU:0 before, /device:TPU:1 now
where the time goes in v2:
time: 34 us; the launch traced here: 33.8 us
  Pallas kernels  20.2 us (59%)
  starting transfers between devices  11 us (32%)
  waiting for transfers between devices  2.16 us (6%)
  loops' own time  0.34 us (1%)
    pallas_call x9, Pallas kernels, call(): pl.pallas_call(body, out_shape=[o if i == result else k(o.shape, o.dtype)...  20.2 us
    ppermute x2, starting transfers between devices, far(): return lax.ppermute(rows, ('peer', 'space'), pairs)  6.51 us
    ppermute x1, starting transfers between devices, exchange(): swap(far_given[1])  1.82 us
    ppermute x2, starting transfers between devices, near(): return lax.ppermute(rows, 'space', pairs)  1.27 us
    ppermute x1, starting transfers between devices, exchange(): swap(near_given[1])  1.21 us
    ppermute x1, waiting for transfers between devices, exchange(): swap(mid_given[1])  1.11 us
    ppermute x2, waiting for transfers between devices, far(): return lax.ppermute(rows, ('peer', 'space'), pairs)  1.04 us
  transfers between devices with their start and end apart: 7, of which 3 were waited for; matrix products, arithmetic and copies ran while one was open for 0% of the time, Pallas kernels for 23%

profile of v2, /device:TPU:1, one launch (start us, length us, event | category | flops | bytes accessed | tf_op | source)
XLA Modules:
  0.0 33.8 jit_solution(10434696776526876728)
XLA Ops:
  0.0 1.3 %prepare.1 = (s32[1]{0:T(128)S(4)}, bf16[16,32,512]{2,1,0:T(8,128)(2,1)S(1)}, bf16[6,32,512]{2,1,0:T(8,128)(2,1)S(1)}, bf16[6,32,512]{2,1,0:T(8,128)(2,1)S(1)}, f32[40,512]{1,0:T(8,128)S(1)}) custom-call(bf16[16,32,512]{2,1,0:T(8,128)(2,1)} %bitcast.44, f32[1,512]{1,0:T(1,128)} %scale1.1, f32[1,512]{1,0:T(1,128)} %shift1.1, f32[1,512]{1,0:T(1,128)} %scale2.1, ...), custom_call_target="tpu_custom_call" | custom-call | flops 72477573120 | tf_op jit(solution)/shard_map/prepare/pallas_call | solution.py:250
  1.3 0.1 collective-permute-start.86
  1.4 2.7 %collective-permute-start.85 = (bf16[6,32,512]{2,1,0:T(8,128)(2,1)S(1)}, bf16[6,32,512]{2,1,0:T(8,128)(2,1)S(1)}, u32[]{:S(2)}, u32[]{:S(2)}) collective-permute-start(bf16[6,32,512]{2,1,0:T(8,128)(2,1)S(1)} %get-tuple-element.759), channel_id=1, source_target_pairs={{0,8},{1,2},{2,1},{3,4},{4,3},{5,6},{6,5},{7,15},{8,0},{9,10},{10,... | collective-permute-start | bytes 589832 | tf_op jit(solution)/shard_map/ppermute | solution.py:329
  4.1 0.0 collective-permute-done.86.near
  4.1 3.4 %first.1 = (bf16[18,32,512]{2,1,0:T(8,128)(2,1)S(1)}, f32[18,32,512]{2,1,0:T(8,128)S(1)}) custom-call(bf16[16,32,512]{2,1,0:T(8,128)(2,1)S(1)} %get-tuple-element.758.image, bf16[6,32,512]{2,1,0:T(8,128)(2,1)S(1)} %collective-permute-done.86.near, bf16[3,1536,512]{2,1,0:T(8,128)(2,1)S(1)} %bitcast.23, f32[40,512]{1,0:T(8,128)S(1)} %get-tuple-element.761.vectors), custom_call_target="tpu_custom_call" | custom-call | flops 2717908992 | tf_op jit(solution)/shard_map/first/pallas_call | solution.py:250
  7.5 0.2 collective-permute-done.85.far
  7.7 4.4 %second.1 = (bf16[6,32,512]{2,1,0:T(8,128)(2,1)S(1)}, bf16[6,32,512]{2,1,0:T(8,128)(2,1)S(1)}, f32[6,32,512]{2,1,0:T(8,128)S(1)}, bf16[6,32,512]{2,1,0:T(8,128)(...) custom-call(bf16[16,32,512]{2,1,0:T(8,128)(2,1)S(1)} %get-tuple-elem, ...), custom_call_target="tpu_custom_call" | custom-call | flops 3321888768 | tf_op jit(solution)/shard_map/second/pallas_call | solution.py:250
  12.1 15.0 %conditional.1 = (bf16[28,32,512]{2,1,0:T(8,128)(2,1)S(1)}, bf16[3,1536,512]{2,1,0:T(8,128)(2,1)S(1)}, bf16[3,1536,512]{2,1,0:T(8,128)(2,1)S(1)}, f32[20,32,512]{2,1,0:T(8,128)S(1)}) conditional(s32[]{:T(128)} %bitcast.1, (bf16[6,32,512]{2,1,0:T(8,128)(2,1)S(1)}, bf16[3,1536,512]{2,1,0:T(8,128)(2,1)}, ...), branch_computations={%region_0.0_spmd, %region_1.0_spmd, %region_2.0_spmd, %region_3.0_... | conditional | flops 2717908992 | bytes 3670248 | solution.py:423
  12.2 1.8 %collective-permute-start.15 = (bf16[6,32,512]{2,1,0:T(8,128)(2,1)S(1)}, bf16[6,32,512]{2,1,0:T(8,128)(2,1)S(1)}, u32[]{:S(2)}, u32[]{:S(2)}) collective-permute-start(bf16[6,32,512]{2,1,0:T(8,128)(2,1)S(1)} %get-tuple-element.499.feat), channel_id=1, source_target_pairs={{0,16},{1,17},{2,18},{3,19},{4,20},{5,21},{6,22},{7,23},{8,0},{9,1... | collective-permute-start | bytes 589832 | tf_op jit(solution)/shard_map/cond/branch_3_fun/ppermute | solution.py:386
  14.0 1.2 %collective-permute-start.18 = (bf16[6,32,512]{2,1,0:T(8,128)(2,1)S(1)}, bf16[6,32,512]{2,1,0:T(8,128)(2,1)S(1)}, u32[]{:S(2)}, u32[]{:S(2)}) collective-permute-start(bf16[6,32,512]{2,1,0:T(8,128)(2,1)S(1)} %get-tuple-element.510.feat), channel_id=1, source_target_pairs={{0,16},{1,17},{2,18},{3,19},{4,20},{5,21},{6,22},{7,23},{8,0},{9,1... | collective-permute-start | bytes 589832 | tf_op jit(solution)/shard_map/cond/branch_3_fun/ppermute | solution.py:386
  15.2 0.2 collective-permute-start.17
  15.4 4.1 %bring.20 = (bf16[3,1536,512]{2,1,0:T(8,128)(2,1)S(1)}, bf16[3,1536,512]{2,1,0:T(8,128)(2,1)S(1)}, f32[20,32,512]{2,1,0:T(8,128)S(1)}, f32[8,128]{1,0:T(8,128)S(1)}) custom-call(bf16[3,1536,512]{2,1,0:T(8,128)(2,1)} %get-tuple-element.502.kernel2, bf16[3,1536,512]{2,1,0:T(8,128)(2,1)} %get-tuple-element.503.kernel1, f32[20,32,512]{2,1,0:T(8,128)} %get-tuple-element.504.fold), custom_call_target="tpu_custom_call" | custom-call | tf_op jit(solution)/shard_map/cond/branch_3_fun/bring/pallas_call | solution.py:250
  19.6 0.0 collective-permute-done.15.partner
  19.6 0.1 grad_first.20.mark.grad_far
  19.7 3.8 %collective-permute-start.16 = (bf16[6,32,512]{2,1,0:T(8,128)(2,1)S(1)}, bf16[6,32,512]{2,1,0:T(8,128)(2,1)S(1)}, u32[]{:S(2)}, u32[]{:S(2)}) collective-permute-start(bf16[6,32,512]{2,1,0:T(8,128)(2,1)S(1)} %grad_first.20.mark.grad_far), channel_id=1, source_target_pairs={{1,2},{2,1},{3,4},{4,3},{5,6},{6,5},{9,10},{10,9},{11,12},{12,11},... | collective-permute-start | bytes 589832 | tf_op jit(solution)/shard_map/cond/branch_3_fun/ppermute | solution.py:329
  23.5 0.0 collective-permute-done.18.partner
  23.5 0.1 grad_near.20
  23.6 1.2 %collective-permute-start.19 = (bf16[6,32,512]{2,1,0:T(8,128)(2,1)S(1)}, bf16[6,32,512]{2,1,0:T(8,128)(2,1)S(1)}, u32[]{:S(2)}, u32[]{:S(2)}) collective-permute-start(bf16[6,32,512]{2,1,0:T(8,128)(2,1)S(1)} %grad_near.20), channel_id=1, source_target_pairs={{0,1},{1,0},{2,3},{3,2},{4,5},{5,4},{6,7},{7,6},{8,9},{9,8},{10,11... | collective-permute-start | bytes 589832 | tf_op jit(solution)/shard_map/cond/branch_3_fun/ppermute | solution.py:326
  24.8 1.1 %collective-permute-done.17.partner = bf16[4,32,512]{2,1,0:T(8,128)(2,1)S(1)} collective-permute-done((bf16[4,32,512]{2,1,0:T(8,128)(2,1)S(1)}, bf16[4,32,512]{2,1,0:T(8,128)(2,1)S(1)}, u32[]{:S(2)}, u32[]{:S(2)}) %collective-permute-start.17) | collective-permute-done | bytes 131104 | tf_op jit(solution)/shard_map/cond/branch_3_fun/ppermute | solution.py:386
  25.9 0.1 grad_mid.20
  26.0 0.0 collective-permute-done.19.near
  26.0 0.9 %collective-permute-done.16.far = bf16[6,32,512]{2,1,0:T(8,128)(2,1)S(1)} collective-permute-done((bf16[6,32,512]{2,1,0:T(8,128)(2,1)S(1)}, bf16[6,32,512]{2,1,0:T(8,128)(2,1)S(1)}, u32[]{:S(2)}, u32[]{:S(2)}) %collective-permute-start.16) | collective-permute-done | bytes 196640 | tf_op jit(solution)/shard_map/cond/branch_3_fun/ppermute | solution.py:329
  26.8 0.1 gather.20
  27.2 6.7 %backward.1 = bf16[16,32,512]{2,1,0:T(8,128)(2,1)} custom-call(bf16[28,32,512]{2,1,0:T(8,128)(2,1)S(1)} %get-tuple-element.774.grads, f32[20,32,512]{2,1,0:T(8,128)S(1)} %get-tuple-element.775.fold, bf16[3,1536,512]{2,1,0:T(8,128)(2,1)S(1)} %get-tuple-element.776.kernel2, bf16[3,1536,512]{2,1,0:T(8,128)(2,1)S(1)} %get-tuple-element.777.kernel1), custom_call_target="tpu_custom_call" | custom-call | flops 5435817984 | tf_op jit(solution)/shard_map/backward/pallas_call | solution.py:250
  (4 shorter events, 0.0 us)
Async XLA Ops:
  0.0 4.1 %copy-start = (bf16[1,3,3,512,512]{4,3,2,1,0:T(8,128)(2,1)S(1)}, bf16[1,3,3,512,512]{4,3,2,1,0:T(8,128)(2,1)}, u32[]{:S(2)}) copy-start(bf16[1,3,3,512,512]{4,3,2,1,0:T(8,128)(2,1)} %param.29) | copy-start | bytes 14155780
  1.3 2.8 %collective-permute-start.86 = (bf16[6,32,512]{2,1,0:T(8,128)(2,1)S(1)}, bf16[6,32,512]{2,1,0:T(8,128)(2,1)S(1)}, u32[]{:S(2)}, u32[]{:S(2)}) collective-permute-start(bf16[6,32,512]{2,1,0:T(8,128)(2,1)S(1)} %get-tuple-element.760), channel_id=1, source_target_pairs={{0,1},{1,0},{2,3},{3,2},{4,5},{5,4},{6,7},{7,6},{8,9},{9,8},{10,11... | collective-permute-start | bytes 589832 | tf_op jit(solution)/shard_map/ppermute | solution.py:326
  1.4 6.3 %collective-permute-start.85 = (bf16[6,32,512]{2,1,0:T(8,128)(2,1)S(1)}, bf16[6,32,512]{2,1,0:T(8,128)(2,1)S(1)}, u32[]{:S(2)}, u32[]{:S(2)}) collective-permute-start(bf16[6,32,512]{2,1,0:T(8,128)(2,1)S(1)} %get-tuple-element.759), channel_id=1, source_target_pairs={{0,8},{1,2},{2,1},{3,4},{4,3},{5,6},{6,5},{7,15},{8,0},{9,10},{10,... | collective-permute-start | bytes 589832 | tf_op jit(solution)/shard_map/ppermute | solution.py:329
  4.1 3.6 %copy-start.1 = (bf16[1,3,3,512,512]{4,3,2,1,0:T(8,128)(2,1)S(1)}, bf16[1,3,3,512,512]{4,3,2,1,0:T(8,128)(2,1)}, u32[]{:S(2)}) copy-start(bf16[1,3,3,512,512]{4,3,2,1,0:T(8,128)(2,1)} %param.32) | copy-start | bytes 14155780
  12.2 7.4 %collective-permute-start.15 = (bf16[6,32,512]{2,1,0:T(8,128)(2,1)S(1)}, bf16[6,32,512]{2,1,0:T(8,128)(2,1)S(1)}, u32[]{:S(2)}, u32[]{:S(2)}) collective-permute-start(bf16[6,32,512]{2,1,0:T(8,128)(2,1)S(1)} %get-tuple-element.499.feat), channel_id=1, source_target_pairs={{0,16},{1,17},{2,18},{3,19},{4,20},{5,21},{6,22},{7,23},{8,0},{9,1... | collective-permute-start | bytes 589832 | tf_op jit(solution)/shard_map/cond/branch_3_fun/ppermute | solution.py:386
  14.0 9.5 %collective-permute-start.18 = (bf16[6,32,512]{2,1,0:T(8,128)(2,1)S(1)}, bf16[6,32,512]{2,1,0:T(8,128)(2,1)S(1)}, u32[]{:S(2)}, u32[]{:S(2)}) collective-permute-start(bf16[6,32,512]{2,1,0:T(8,128)(2,1)S(1)} %get-tuple-element.510.feat), channel_id=1, source_target_pairs={{0,16},{1,17},{2,18},{3,19},{4,20},{5,21},{6,22},{7,23},{8,0},{9,1... | collective-permute-start | bytes 589832 | tf_op jit(solution)/shard_map/cond/branch_3_fun/ppermute | solution.py:386
  15.2 10.7 %collective-permute-start.17 = (bf16[4,32,512]{2,1,0:T(8,128)(2,1)S(1)}, bf16[4,32,512]{2,1,0:T(8,128)(2,1)S(1)}, u32[]{:S(2)}, u32[]{:S(2)}) collective-permute-start(bf16[4,32,512]{2,1,0:T(8,128)(2,1)S(1)} %get-tuple-element.507.feat), channel_id=1, source_target_pairs={{0,16},{1,17},{2,18},{3,19},{4,20},{5,21},{6,22},{7,23},{8,0},{9,1... | collective-permute-start | bytes 393224 | tf_op jit(solution)/shard_map/cond/branch_3_fun/ppermute | solution.py:386
  19.7 7.1 %collective-permute-start.16 = (bf16[6,32,512]{2,1,0:T(8,128)(2,1)S(1)}, bf16[6,32,512]{2,1,0:T(8,128)(2,1)S(1)}, u32[]{:S(2)}, u32[]{:S(2)}) collective-permute-start(bf16[6,32,512]{2,1,0:T(8,128)(2,1)S(1)} %grad_first.20.mark.grad_far), channel_id=1, source_target_pairs={{1,2},{2,1},{3,4},{4,3},{5,6},{6,5},{9,10},{10,9},{11,12},{12,11},... | collective-permute-start | bytes 589832 | tf_op jit(solution)/shard_map/cond/branch_3_fun/ppermute | solution.py:329
  23.6 2.3 %collective-permute-start.19 = (bf16[6,32,512]{2,1,0:T(8,128)(2,1)S(1)}, bf16[6,32,512]{2,1,0:T(8,128)(2,1)S(1)}, u32[]{:S(2)}, u32[]{:S(2)}) collective-permute-start(bf16[6,32,512]{2,1,0:T(8,128)(2,1)S(1)} %grad_near.20), channel_id=1, source_target_pairs={{0,1},{1,0},{2,3},{3,2},{4,5},{5,4},{6,7},{7,6},{8,9},{9,8},{10,11... | collective-permute-start | bytes 589832 | tf_op jit(solution)/shard_map/cond/branch_3_fun/ppermute | solution.py:326

commit v3 on v2

--- a/solution.py
+++ b/solution.py
@@ -383,7 +383,7 @@
 
     def exchange(swap, *given):
         far_given, near_given, mid_given, (vectors, *stored) = given[:3], given[3:6], given[6:9], given[9:]
-        partner_far, partner_near, partner_mid = swap(far_given[1]), swap(near_given[1]), swap(mid_given[1])
+        partner_far, partner_near = swap(far_given[1]), swap(near_given[1])
         *brought, mark = call(
             bring,
             "bring",
@@ -392,6 +392,8 @@
             (dma((3,)),),
             remote=range(3),
         )
+        partner_far, feat_mid, mark = lax.optimization_barrier((partner_far, mid_given[1], mark))
+        partner_mid = swap(feat_mid)
         (grad_far,) = call(
             grad_first,
             "grad_first",

time: 34 us -> 35.7 us (1.050)
  waiting for transfers between devices: 2.16 us -> 3.24 us
  starting transfers between devices: 11 us -> 11.5 us
    ppermute x2, starting transfers between devices: 1.27 us -> 0.19 us  [near(): return lax.ppermute(rows, 'space', pairs)]
    ppermute x2, starting transfers between devices: 6.51 us -> 7.56 us  [far(): return lax.ppermute(rows, ('peer', 'space'), pairs)]
    ppermute x2, waiting for transfers between devices: 1.04 us -> 1.88 us  [far(): return lax.ppermute(rows, ('peer', 'space'), pairs)]
    ppermute x2, waiting for transfers between devices: 0.01 us -> 0.69 us  [near(): return lax.ppermute(rows, 'space', pairs)]
    ppermute x3, starting transfers between devices: 3.26 us -> 3.73 us  [the longest x2 3.03 us: exchange(): partner_far, partner_near = (swap(far_given[1]), swap(near_given[1]))]
    ppermute x3, waiting for transfers between devices: 1.11 us -> 0.66 us  [the longest x1 0.66 us: exchange(): partner_mid = swap(feat_mid)]
  transfers between devices with their start and end apart: 7 -> 7, of which waited for: 3 -> 4; matrix products, arithmetic and copies ran while one was open for 0% -> 0% of each run, Pallas kernels for 23% -> 22%
where the time goes in v3:
time: 35.7 us; the launch traced here: 35.3 us
  Pallas kernels  20.2 us (57%)
  starting transfers between devices  11.5 us (32%)
  waiting for transfers between devices  3.24 us (9%)
    pallas_call x9, Pallas kernels, call(): pl.pallas_call(body, out_shape=[o if i == result else k(o.shape, o.dtype)...  20.2 us
    ppermute x2, starting transfers between devices, far(): return lax.ppermute(rows, ('peer', 'space'), pairs)  7.56 us
    ppermute x2, starting transfers between devices, exchange(): partner_far, partner_near = (swap(far_given[1]), swap(near_given[1]))  3.03 us
    ppermute x2, waiting for transfers between devices, far(): return lax.ppermute(rows, ('peer', 'space'), pairs)  1.88 us
  transfers between devices with their start and end apart: 7, of which 4 were waited for; matrix products, arithmetic and copies ran while one was open for 0% of the time, Pallas kernels for 22%

profile of v3, /device:TPU:1, one launch (start us, length us, event | category | flops | bytes accessed | tf_op | source)
XLA Modules:
  0.0 35.3 jit_solution(6172791032686667924)
XLA Ops:
  0.0 1.3 %prepare.1 = (s32[1]{0:T(128)S(4)}, bf16[16,32,512]{2,1,0:T(8,128)(2,1)S(1)}, bf16[6,32,512]{2,1,0:T(8,128)(2,1)S(1)}, bf16[6,32,512]{2,1,0:T(8,128)(2,1)S(1)}, f32[40,512]{1,0:T(8,128)S(1)}) custom-call(bf16[16,32,512]{2,1,0:T(8,128)(2,1)} %bitcast.44, f32[1,512]{1,0:T(1,128)} %scale1.1, f32[1,512]{1,0:T(1,128)} %shift1.1, f32[1,512]{1,0:T(1,128)} %scale2.1, ...), custom_call_target="tpu_custom_call" | custom-call | flops 72477573120 | tf_op jit(solution)/shard_map/prepare/pallas_call | solution.py:250
  1.3 0.1 collective-permute-start.86
  1.4 2.7 %collective-permute-start.85 = (bf16[6,32,512]{2,1,0:T(8,128)(2,1)S(1)}, bf16[6,32,512]{2,1,0:T(8,128)(2,1)S(1)}, u32[]{:S(2)}, u32[]{:S(2)}) collective-permute-start(bf16[6,32,512]{2,1,0:T(8,128)(2,1)S(1)} %get-tuple-element.810), channel_id=1, source_target_pairs={{0,8},{1,2},{2,1},{3,4},{4,3},{5,6},{6,5},{7,15},{8,0},{9,10},{10,... | collective-permute-start | bytes 589832 | tf_op jit(solution)/shard_map/ppermute | solution.py:329
  4.1 0.0 collective-permute-done.86.near
  4.1 3.4 %first.1 = (bf16[18,32,512]{2,1,0:T(8,128)(2,1)S(1)}, f32[18,32,512]{2,1,0:T(8,128)S(1)}) custom-call(bf16[16,32,512]{2,1,0:T(8,128)(2,1)S(1)} %get-tuple-element.809.image, bf16[6,32,512]{2,1,0:T(8,128)(2,1)S(1)} %collective-permute-done.86.near, bf16[3,1536,512]{2,1,0:T(8,128)(2,1)S(1)} %bitcast.23, f32[40,512]{1,0:T(8,128)S(1)} %get-tuple-element.812.vectors), custom_call_target="tpu_custom_call" | custom-call | flops 2717908992 | tf_op jit(solution)/shard_map/first/pallas_call | solution.py:250
  7.5 0.2 collective-permute-done.85.far
  7.7 4.4 %second.1 = (bf16[6,32,512]{2,1,0:T(8,128)(2,1)S(1)}, bf16[6,32,512]{2,1,0:T(8,128)(2,1)S(1)}, f32[6,32,512]{2,1,0:T(8,128)S(1)}, bf16[6,32,512]{2,1,0:T(8,128)(...) custom-call(bf16[16,32,512]{2,1,0:T(8,128)(2,1)S(1)} %get-tuple-elem, ...), custom_call_target="tpu_custom_call" | custom-call | flops 3321888768 | tf_op jit(solution)/shard_map/second/pallas_call | solution.py:250
  12.1 16.5 %conditional.1 = (bf16[28,32,512]{2,1,0:T(8,128)(2,1)S(1)}, bf16[3,1536,512]{2,1,0:T(8,128)(2,1)S(1)}, bf16[3,1536,512]{2,1,0:T(8,128)(2,1)S(1)}, f32[20,32,512]{2,1,0:T(8,128)S(1)}) conditional(s32[]{:T(128)} %bitcast.1, (bf16[6,32,512]{2,1,0:T(8,128)(2,1)S(1)}, bf16[3,1536,512]{2,1,0:T(8,128)(2,1)}, ...), branch_computations={%region_0.0_spmd, %region_1.0_spmd, %region_2.0_spmd, %region_3.0_... | conditional | flops 2717908992 | bytes 3670248 | solution.py:425
  12.2 1.8 %collective-permute-start.15 = (bf16[6,32,512]{2,1,0:T(8,128)(2,1)S(1)}, bf16[6,32,512]{2,1,0:T(8,128)(2,1)S(1)}, u32[]{:S(2)}, u32[]{:S(2)}) collective-permute-start(bf16[6,32,512]{2,1,0:T(8,128)(2,1)S(1)} %get-tuple-element.508.feat), channel_id=1, source_target_pairs={{0,16},{1,17},{2,18},{3,19},{4,20},{5,21},{6,22},{7,23},{8,0},{9,1... | collective-permute-start | bytes 589832 | tf_op jit(solution)/shard_map/cond/branch_3_fun/ppermute | solution.py:386
  14.0 1.2 %collective-permute-start.18 = (bf16[6,32,512]{2,1,0:T(8,128)(2,1)S(1)}, bf16[6,32,512]{2,1,0:T(8,128)(2,1)S(1)}, u32[]{:S(2)}, u32[]{:S(2)}) collective-permute-start(bf16[6,32,512]{2,1,0:T(8,128)(2,1)S(1)} %get-tuple-element.522.feat), channel_id=1, source_target_pairs={{0,16},{1,17},{2,18},{3,19},{4,20},{5,21},{6,22},{7,23},{8,0},{9,1... | collective-permute-start | bytes 589832 | tf_op jit(solution)/shard_map/cond/branch_3_fun/ppermute | solution.py:386
  15.2 4.1 %bring.20 = (bf16[3,1536,512]{2,1,0:T(8,128)(2,1)S(1)}, bf16[3,1536,512]{2,1,0:T(8,128)(2,1)S(1)}, f32[20,32,512]{2,1,0:T(8,128)S(1)}, f32[8,128]{1,0:T(8,128)S(1)}) custom-call(bf16[3,1536,512]{2,1,0:T(8,128)(2,1)} %get-tuple-element.511.kernel2, bf16[3,1536,512]{2,1,0:T(8,128)(2,1)} %get-tuple-element.512.kernel1, f32[20,32,512]{2,1,0:T(8,128)} %get-tuple-element.513.fold), custom_call_target="tpu_custom_call" | custom-call | tf_op jit(solution)/shard_map/cond/branch_3_fun/bring/pallas_call | solution.py:250
  19.3 0.0 collective-permute-done.15.partner
  19.3 0.7 %collective-permute-start.17 = (bf16[4,32,512]{2,1,0:T(8,128)(2,1)S(1)}, bf16[4,32,512]{2,1,0:T(8,128)(2,1)S(1)}, u32[]{:S(2)}, u32[]{:S(2)}) collective-permute-start(bf16[4,32,512]{2,1,0:T(8,128)(2,1)S(1)} %get-tuple-element.520.feat), channel_id=1, source_target_pairs={{0,16},{1,17},{2,18},{3,19},{4,20},{5,21},{6,22},{7,23},{8,0},{9,1... | collective-permute-start | bytes 393224 | tf_op jit(solution)/shard_map/cond/branch_3_fun/ppermute | solution.py:396
  20.0 0.1 grad_first.20.mark.grad_far
  20.2 4.9 %collective-permute-start.16 = (bf16[6,32,512]{2,1,0:T(8,128)(2,1)S(1)}, bf16[6,32,512]{2,1,0:T(8,128)(2,1)S(1)}, u32[]{:S(2)}, u32[]{:S(2)}) collective-permute-start(bf16[6,32,512]{2,1,0:T(8,128)(2,1)S(1)} %grad_first.20.mark.grad_far), channel_id=1, source_target_pairs={{1,2},{2,1},{3,4},{4,3},{5,6},{6,5},{9,10},{10,9},{11,12},{12,11},... | collective-permute-start | bytes 589832 | tf_op jit(solution)/shard_map/cond/branch_3_fun/ppermute | solution.py:329
  25.0 0.0 collective-permute-done.18.partner
  25.0 0.1 grad_near.20
  25.2 0.1 collective-permute-start.19
  25.2 0.7 %collective-permute-done.17.partner = bf16[4,32,512]{2,1,0:T(8,128)(2,1)S(1)} collective-permute-done((bf16[4,32,512]{2,1,0:T(8,128)(2,1)S(1)}, bf16[4,32,512]{2,1,0:T(8,128)(2,1)S(1)}, u32[]{:S(2)}, u32[]{:S(2)}) %collective-permute-start.17) | collective-permute-done | bytes 131104 | tf_op jit(solution)/shard_map/cond/branch_3_fun/ppermute | solution.py:396
  25.9 0.1 grad_mid.20
  26.0 0.7 %collective-permute-done.19.near = bf16[6,32,512]{2,1,0:T(8,128)(2,1)S(1)} collective-permute-done((bf16[6,32,512]{2,1,0:T(8,128)(2,1)S(1)}, bf16[6,32,512]{2,1,0:T(8,128)(2,1)S(1)}, u32[]{:S(2)}, u32[]{:S(2)}) %collective-permute-start.19) | collective-permute-done | bytes 196640 | tf_op jit(solution)/shard_map/cond/branch_3_fun/ppermute | solution.py:326
  26.7 1.7 %collective-permute-done.16.far = bf16[6,32,512]{2,1,0:T(8,128)(2,1)S(1)} collective-permute-done((bf16[6,32,512]{2,1,0:T(8,128)(2,1)S(1)}, bf16[6,32,512]{2,1,0:T(8,128)(2,1)S(1)}, u32[]{:S(2)}, u32[]{:S(2)}) %collective-permute-start.16) | collective-permute-done | bytes 196640 | tf_op jit(solution)/shard_map/cond/branch_3_fun/ppermute | solution.py:329
  28.4 0.1 gather.20
  28.7 6.7 %backward.1 = bf16[16,32,512]{2,1,0:T(8,128)(2,1)} custom-call(bf16[28,32,512]{2,1,0:T(8,128)(2,1)S(1)} %get-tuple-element.825.grads, f32[20,32,512]{2,1,0:T(8,128)S(1)} %get-tuple-element.826.fold, bf16[3,1536,512]{2,1,0:T(8,128)(2,1)S(1)} %get-tuple-element.827.kernel2, bf16[3,1536,512]{2,1,0:T(8,128)(2,1)S(1)} %get-tuple-element.828.kernel1), custom_call_target="tpu_custom_call" | custom-call | flops 5435817984 | tf_op jit(solution)/shard_map/backward/pallas_call | solution.py:250
  (4 shorter events, 0.0 us)
Async XLA Ops:
  0.0 4.1 %copy-start = (bf16[1,3,3,512,512]{4,3,2,1,0:T(8,128)(2,1)S(1)}, bf16[1,3,3,512,512]{4,3,2,1,0:T(8,128)(2,1)}, u32[]{:S(2)}) copy-start(bf16[1,3,3,512,512]{4,3,2,1,0:T(8,128)(2,1)} %param.29) | copy-start | bytes 14155780
  1.3 2.8 %collective-permute-start.86 = (bf16[6,32,512]{2,1,0:T(8,128)(2,1)S(1)}, bf16[6,32,512]{2,1,0:T(8,128)(2,1)S(1)}, u32[]{:S(2)}, u32[]{:S(2)}) collective-permute-start(bf16[6,32,512]{2,1,0:T(8,128)(2,1)S(1)} %get-tuple-element.811), channel_id=1, source_target_pairs={{0,1},{1,0},{2,3},{3,2},{4,5},{5,4},{6,7},{7,6},{8,9},{9,8},{10,11... | collective-permute-start | bytes 589832 | tf_op jit(solution)/shard_map/ppermute | solution.py:326
  1.4 6.3 %collective-permute-start.85 = (bf16[6,32,512]{2,1,0:T(8,128)(2,1)S(1)}, bf16[6,32,512]{2,1,0:T(8,128)(2,1)S(1)}, u32[]{:S(2)}, u32[]{:S(2)}) collective-permute-start(bf16[6,32,512]{2,1,0:T(8,128)(2,1)S(1)} %get-tuple-element.810), channel_id=1, source_target_pairs={{0,8},{1,2},{2,1},{3,4},{4,3},{5,6},{6,5},{7,15},{8,0},{9,10},{10,... | collective-permute-start | bytes 589832 | tf_op jit(solution)/shard_map/ppermute | solution.py:329
  4.1 3.6 %copy-start.1 = (bf16[1,3,3,512,512]{4,3,2,1,0:T(8,128)(2,1)S(1)}, bf16[1,3,3,512,512]{4,3,2,1,0:T(8,128)(2,1)}, u32[]{:S(2)}) copy-start(bf16[1,3,3,512,512]{4,3,2,1,0:T(8,128)(2,1)} %param.32) | copy-start | bytes 14155780
  12.2 7.2 %collective-permute-start.15 = (bf16[6,32,512]{2,1,0:T(8,128)(2,1)S(1)}, bf16[6,32,512]{2,1,0:T(8,128)(2,1)S(1)}, u32[]{:S(2)}, u32[]{:S(2)}) collective-permute-start(bf16[6,32,512]{2,1,0:T(8,128)(2,1)S(1)} %get-tuple-element.508.feat), channel_id=1, source_target_pairs={{0,16},{1,17},{2,18},{3,19},{4,20},{5,21},{6,22},{7,23},{8,0},{9,1... | collective-permute-start | bytes 589832 | tf_op jit(solution)/shard_map/cond/branch_3_fun/ppermute | solution.py:386
  14.0 11.0 %collective-permute-start.18 = (bf16[6,32,512]{2,1,0:T(8,128)(2,1)S(1)}, bf16[6,32,512]{2,1,0:T(8,128)(2,1)S(1)}, u32[]{:S(2)}, u32[]{:S(2)}) collective-permute-start(bf16[6,32,512]{2,1,0:T(8,128)(2,1)S(1)} %get-tuple-element.522.feat), channel_id=1, source_target_pairs={{0,16},{1,17},{2,18},{3,19},{4,20},{5,21},{6,22},{7,23},{8,0},{9,1... | collective-permute-start | bytes 589832 | tf_op jit(solution)/shard_map/cond/branch_3_fun/ppermute | solution.py:386
  19.3 6.5 %collective-permute-start.17 = (bf16[4,32,512]{2,1,0:T(8,128)(2,1)S(1)}, bf16[4,32,512]{2,1,0:T(8,128)(2,1)S(1)}, u32[]{:S(2)}, u32[]{:S(2)}) collective-permute-start(bf16[4,32,512]{2,1,0:T(8,128)(2,1)S(1)} %get-tuple-element.520.feat), channel_id=1, source_target_pairs={{0,16},{1,17},{2,18},{3,19},{4,20},{5,21},{6,22},{7,23},{8,0},{9,1... | collective-permute-start | bytes 393224 | tf_op jit(solution)/shard_map/cond/branch_3_fun/ppermute | solution.py:396
  20.2 8.2 %collective-permute-start.16 = (bf16[6,32,512]{2,1,0:T(8,128)(2,1)S(1)}, bf16[6,32,512]{2,1,0:T(8,128)(2,1)S(1)}, u32[]{:S(2)}, u32[]{:S(2)}) collective-permute-start(bf16[6,32,512]{2,1,0:T(8,128)(2,1)S(1)} %grad_first.20.mark.grad_far), channel_id=1, source_target_pairs={{1,2},{2,1},{3,4},{4,3},{5,6},{6,5},{9,10},{10,9},{11,12},{12,11},... | collective-permute-start | bytes 589832 | tf_op jit(solution)/shard_map/cond/branch_3_fun/ppermute | solution.py:329
  25.2 1.5 %collective-permute-start.19 = (bf16[6,32,512]{2,1,0:T(8,128)(2,1)S(1)}, bf16[6,32,512]{2,1,0:T(8,128)(2,1)S(1)}, u32[]{:S(2)}, u32[]{:S(2)}) collective-permute-start(bf16[6,32,512]{2,1,0:T(8,128)(2,1)S(1)} %grad_near.20), channel_id=1, source_target_pairs={{0,1},{1,0},{2,3},{3,2},{4,5},{5,4},{6,7},{7,6},{8,9},{9,8},{10,11... | collective-permute-start | bytes 589832 | tf_op jit(solution)/shard_map/cond/branch_3_fun/ppermute | solution.py:326
